TPU v7x, 512 devices: a whole 4x8x8 slice. The times are simulated.
512 devices in a mesh: learn: 32 (over z, y_lo), rep: 2 (over core), tp: 8 (over x, y_hi).
Axes of the slice: x: 4, y: 8 (y_hi: 2, y_lo: 4; y = y_hi * 4 + y_lo), z: 8, core: 2. Of those that a mesh axis runs over, the one named last changes fastest.
Arguments:
- master: float32 [5120, 8, 1280], P(('learn', 'rep'), 'tp'), may hold values from -6 to 6
- adam_first_moment: float32 [5120, 8, 1280], P(('learn', 'rep'), 'tp'), may hold values from -6 to 6
- adam_second_moment: float32 [5120, 8, 1280], P(('learn', 'rep'), 'tp'), may hold values from 0.05 to 1
- gradient: bfloat16 [5120, 8, 1280], P(('learn', 'rep'), 'tp'), may hold values from -6 to 6
- resync_order: int32 [64], replicated, may hold values from 0 to 63, each once
- inputs: bfloat16 [4, 128, 5120], P(None, ('learn', 'rep')), may hold values from -0.3125 to 0.3125
- in_gain: float32 [5120], replicated, may hold values from 0.1 to 1.9
- post_gain: float32 [5120], P('tp'), may hold values from 0.1 to 1.9
- lengths: int32 [128], P(('learn', 'rep')), may hold values from 256 to 2044, as said below
- cached_key_rows: bfloat16 [128, 8, 2048, 128], P(('learn', 'rep'), 'tp'), may hold values from -6 to 6
- cached_value_rows: bfloat16 [128, 8, 2048, 128], P(('learn', 'rep'), 'tp'), may hold values from -6 to 6
Outputs:
- new_master: float32 [5120, 8, 1280], P(('learn', 'rep'), 'tp')
- mixed: bfloat16 [4, 128, 5120], P(None, ('learn', 'rep'), 'tp')
Inputs may be any that keep to these rules, and one draw needn't show every extreme that they name: `resync_order`: a permutation of the 64 row blocks. `lengths`: some row has exactly 2044 cached tokens.
All inputs are finite; a program needn't handle non-finite values.
Results may differ from a plain program's by a relative error of at most 0.018.
Values may be sent and summed in bfloat16 or wider, within the bound.
A program may use at most 64 MiB of HBM per device.

v0:
```python
import jax
import jax.numpy as jnp
from jax import lax
from jax.sharding import PartitionSpec as P

MODEL_WIDTH = 5120
HEAD_SIZE = 128
KEY_VALUE_HEADS = 8
QUERY_PER_GROUP = 4
STEPS = 4


beta_one = 0.9
beta_two = 0.95
adam_rate = 0.05
adam_decay = 0.1
adam_epsilon = 1e-08
correction_one = 1.0 - 0.9**10
correction_two = 1.0 - 0.95**10
norm_epsilon = 1e-06
rope_theta = 1000000.0


def adam_update(master, adam_first_moment, adam_second_moment, gradient):
    gradient_wide = gradient.astype(jnp.float32)
    first_moment = beta_one * adam_first_moment + (1.0 - beta_one) * gradient_wide
    second_moment = beta_two * adam_second_moment + (1.0 - beta_two) * gradient_wide * gradient_wide
    update = (
        first_moment / correction_one / (jnp.sqrt(second_moment / correction_two) + adam_epsilon)
        + adam_decay * master
    )
    return master - adam_rate * update


def inverse_order(order):
    places = jnp.arange(order.shape[0], dtype=jnp.int32)
    return jnp.sum(jnp.where(order[None, :] == places[:, None], places[None, :], 0), axis=1)


def head_norm_gain(values):
    return values * lax.rsqrt(jnp.mean(values * values, axis=-1, keepdims=True) + norm_epsilon)


def rotate(values, positions):
    half_size = values.shape[-1] // 2
    freqs = rope_theta ** (-(jnp.arange(half_size, dtype=jnp.float32) * 2.0 / values.shape[-1]))
    angles = positions.astype(jnp.float32)[:, None] * freqs[None, :]
    cosine = jnp.cos(angles)[:, None, None, :]
    sine = jnp.sin(angles)[:, None, None, :]
    front_half = values[..., :half_size]
    back_half = values[..., half_size:]
    return jnp.concatenate(
        [front_half * cosine - back_half * sine, back_half * cosine + front_half * sine], axis=-1
    )


def attend(query_rows, recent_keys, recent_values, cached_key_rows, cached_value_rows, lengths):
    scale = HEAD_SIZE ** (-0.5)
    past_scores = (
        jnp.einsum(
            "ngqh,ngph->ngqp", query_rows, cached_key_rows, preferred_element_type=jnp.float32
        )
        * scale
    )
    live_mask = jnp.arange(cached_key_rows.shape[2], dtype=jnp.int32)[None, :] < lengths[:, None]
    past_exp = jnp.where(live_mask[:, None, None, :], jnp.exp(past_scores), 0.0)
    recent_scores = (
        jnp.einsum("ngqh,ngph->ngqp", query_rows, recent_keys, preferred_element_type=jnp.float32)
        * scale
    )
    recent_exp = jnp.exp(recent_scores)
    denominator = jnp.sum(past_exp, axis=-1, keepdims=True) + jnp.sum(
        recent_exp, axis=-1, keepdims=True
    )
    past_weights = (past_exp / denominator).astype(jnp.bfloat16)
    recent_weights = (recent_exp / denominator).astype(jnp.bfloat16)
    head_split = jnp.einsum(
        "ngqp,ngph->ngqh", past_weights, cached_value_rows, preferred_element_type=jnp.float32
    )
    head_split = head_split + jnp.einsum(
        "ngqp,ngph->ngqh", recent_weights, recent_values, preferred_element_type=jnp.float32
    )
    return head_split.astype(jnp.bfloat16)


def body(
    master,
    adam_first_moment,
    adam_second_moment,
    gradient,
    resync_order,
    inputs,
    in_gain,
    post_gain,
    lengths,
    cached_key_rows,
    cached_value_rows,
):
    new_master = adam_update(master, adam_first_moment, adam_second_moment, gradient)
    fresh_token = new_master.astype(jnp.bfloat16)
    gathered = lax.all_gather(fresh_token, ("learn", "rep"), axis=0, tiled=True)
    shards = lax.axis_size("learn") * lax.axis_size("rep")
    row_block = MODEL_WIDTH // shards
    groups = gathered.shape[1]
    query_columns = QUERY_PER_GROUP * HEAD_SIZE
    weights_in = gathered[:, :, : query_columns + 2 * HEAD_SIZE]
    output_weight_matrix = gathered[:, :, query_columns + 2 * HEAD_SIZE :]
    inverse_index = inverse_order(resync_order)
    count_of_rows = inputs.shape[1]
    in_scale = 1.0 / jnp.sqrt(jnp.float32(MODEL_WIDTH))
    output_scale_factor = 1.0 / jnp.sqrt(jnp.float32(KEY_VALUE_HEADS * query_columns))
    keys_so_far = []
    values_so_far = []
    attn_steps = []
    for step_index in range(STEPS):
        stream = inputs[step_index].astype(jnp.float32)
        normed_in = (
            stream
            * lax.rsqrt(jnp.mean(stream * stream, axis=-1, keepdims=True) + norm_epsilon)
            * in_gain
        ).astype(jnp.bfloat16)
        stored_order = jnp.take(
            normed_in.reshape(count_of_rows, shards, row_block), resync_order, axis=1
        ).reshape(count_of_rows, MODEL_WIDTH)
        projected_input = (
            jnp.einsum("nd,dgc->ngc", stored_order, weights_in, preferred_element_type=jnp.float32)
            * in_scale
        )
        query_rows = head_norm_gain(
            projected_input[:, :, :query_columns].reshape(
                count_of_rows, groups, QUERY_PER_GROUP, HEAD_SIZE
            )
        )
        latest_keys = head_norm_gain(
            projected_input[:, :, query_columns : query_columns + HEAD_SIZE].reshape(
                count_of_rows, groups, 1, HEAD_SIZE
            )
        )
        latest_values = (
            projected_input[:, :, query_columns + HEAD_SIZE :]
            .reshape(count_of_rows, groups, 1, HEAD_SIZE)
            .astype(jnp.bfloat16)
        )
        positions = lengths + step_index
        query_rows = rotate(query_rows, positions).astype(jnp.bfloat16)
        latest_keys = rotate(latest_keys, positions).astype(jnp.bfloat16)
        keys_so_far.append(latest_keys)
        values_so_far.append(latest_values)
        recent_keys = jnp.concatenate(keys_so_far, axis=2)
        recent_values = jnp.concatenate(values_so_far, axis=2)
        head_split = attend(
            query_rows, recent_keys, recent_values, cached_key_rows, cached_value_rows, lengths
        )
        head_split = head_split.reshape(count_of_rows, groups, query_columns)
        stored_attn = (
            jnp.einsum(
                "bae,oae->bo", head_split, output_weight_matrix, preferred_element_type=jnp.float32
            )
            * output_scale_factor
        )
        attention_output = jnp.take(
            stored_attn.reshape(count_of_rows, shards, row_block), inverse_index, axis=1
        ).reshape(count_of_rows, MODEL_WIDTH)
        attn_steps.append(attention_output)
    attn_all = jnp.stack(attn_steps)
    stream_all = inputs.astype(jnp.float32)
    slab_width = MODEL_WIDTH // lax.axis_size("tp")
    slab_start = lax.axis_index("tp") * slab_width
    summed = lax.psum(attn_all.astype(jnp.bfloat16), "tp").astype(jnp.float32)
    residual = stream_all + summed
    normed_full = residual * lax.rsqrt(
        jnp.mean(residual * residual, axis=2, keepdims=True) + norm_epsilon
    )
    normed_out = lax.dynamic_slice_in_dim(normed_full, slab_start, slab_width, 2)
    return (new_master, (normed_out * post_gain).astype(jnp.bfloat16))


def solution(mesh):
    in_specs = (
        P(("learn", "rep"), "tp", None),
        P(("learn", "rep"), "tp", None),
        P(("learn", "rep"), "tp", None),
        P(("learn", "rep"), "tp", None),
        P(),
        P(None, ("learn", "rep"), None),
        P(),
        P("tp"),
        P(("learn", "rep")),
        P(("learn", "rep"), "tp", None, None),
        P(("learn", "rep"), "tp", None, None),
    )
    out_specs = (P(("learn", "rep"), "tp", None), P(None, ("learn", "rep"), "tp"))
    return jax.shard_map(body, mesh=mesh, in_specs=in_specs, out_specs=out_specs, check_vma=False)
```

profile of v0, /device:TPU:6, one launch (start us, length us, event | category | flops | bytes accessed | tf_op | source)
XLA Modules:
  0.0 297.3 jit_solution(879844079533895067)
XLA Ops:
  7.2 2.4 fusion.127
  9.7 0.8 mul.749
  10.5 0.8 slice_convert_fusion.3
  11.8 1.0 multiply_reduce_fusion.4
  13.1 0.7 compare_select_fusion.1
  13.8 0.6 gather_fusion
  14.4 0.6 gather_fusion.2
  15.1 0.6 gather_fusion.4
  15.8 0.6 gather_fusion.6
  16.4 0.7 compare_and_fusion.1
  17.1 0.2 fusion.56
  17.9 0.8 select_reduce_fusion
  18.7 0.7 fusion.129
  19.6 0.7 iota_compare_fusion.1
  20.3 125.6 %all-gather.2.cloned.1.call-done = bf16[5120,1,1280]{2,0,1:T(8,128)(2,1)} async-done(((bf16[80,1,1280]{2,0,1:T(8,128)(2,1)}), bf16[5120,1,1280]{2,0,1:T(8,128)(2,1)}) %all-gather.2.cloned.1.call-update) | async-done | bytes 13107216 | tf_op jit(solution)/shard_map/all_gather | solution.py:101
  145.9 4.5 %fusion.21 = f32[2,1,768]{2,0,1:T(2,128)S(1)} fusion(bf16[2,5120]{1,0:T(2,128)(2,1)S(1)} %reshape.1401, bf16[5120,1,1280]{2,0,1:T(8,128)(2,1)} %all-gather.2.cloned.1.call-done), kind=kOutput, calls=%fused_computation.45 | convolution fusion | flops 15730176 | bytes 7890944 | tf_op jit(solution)/shard_map/nd,dgc->ngc/dot_general | solution.py:126
  150.6 5.1 %fusion.19 = f32[2,1,768]{2,0,1:T(2,128)S(1)} fusion(bf16[2,5120]{1,0:T(2,128)(2,1)S(1)} %reshape.1394, bf16[5120,1,1280]{2,0,1:T(8,128)(2,1)} %all-gather.2.cloned.1.call-done), kind=kOutput, calls=%fused_computation.43 | convolution fusion | flops 15730176 | bytes 7890944 | tf_op jit(solution)/shard_map/nd,dgc->ngc/dot_general | solution.py:126
  155.8 1.1 fusion.17
  157.1 1.1 fusion.15
  159.9 0.2 fusion.119
  160.1 0.5 fusion.130
  160.6 0.5 fusion.131
  161.1 0.2 fusion.132
  161.6 0.5 fusion.135
  162.1 0.2 fusion.136
  162.3 0.5 fusion.133
  162.8 0.2 fusion.134
  163.1 0.3 fusion.33
  163.4 0.2 fusion.27
  163.6 4.0 %convolution_multiply_fusion.1 = bf16[2,5120]{1,0:T(2,128)(2,1)S(1)} fusion(bf16[5120,1,1280]{2,0,1:T(8,128)(2,1)} %all-gather.2.cloned.1.call-done, bf16[1,2,4,128]{3,2,1,0:T(4,128)(2,1)S(1)} %fusion.27), kind=kOutput, calls=%fused_computation.10 | convolution fusion | flops 10506240 | bytes 5265408 | tf_op jit(solution)/shard_map/bae,oae->bo/dot_general | solution.py:156
  167.8 0.3 fusion.31
  168.1 0.2 fusion.26
  168.3 3.9 %convolution_multiply_fusion = bf16[2,5120]{1,0:T(2,128)(2,1)S(1)} fusion(bf16[5120,1,1280]{2,0,1:T(8,128)(2,1)} %all-gather.2.cloned.1.call-done, bf16[1,2,4,128]{3,2,1,0:T(4,128)(2,1)S(1)} %fusion.26), kind=kOutput, calls=%fused_computation.9 | convolution fusion | flops 10506240 | bytes 5265408 | tf_op jit(solution)/shard_map/bae,oae->bo/dot_general | solution.py:156
  172.4 0.6 gather_fusion.5
  173.0 0.6 gather_fusion.7
  173.7 0.3 fusion.35
  174.0 0.2 fusion.28
  174.2 3.9 %convolution_multiply_fusion.2 = bf16[2,5120]{1,0:T(2,128)(2,1)S(1)} fusion(bf16[5120,1,1280]{2,0,1:T(8,128)(2,1)} %all-gather.2.cloned.1.call-done, bf16[1,2,4,128]{3,2,1,0:T(4,128)(2,1)S(1)} %fusion.28), kind=kOutput, calls=%fused_computation.11 | convolution fusion | flops 10506240 | bytes 5265408 | tf_op jit(solution)/shard_map/bae,oae->bo/dot_general | solution.py:156
  178.3 0.6 gather_fusion.3
  179.0 0.3 fusion.29
  179.3 4.0 %convolution_multiply_fusion.3 = bf16[2,5120]{1,0:T(2,128)(2,1)S(1)} fusion(bf16[5120,1,1280]{2,0,1:T(8,128)(2,1)} %all-gather.2.cloned.1.call-done, bf16[1,2,4,128]{3,2,1,0:T(4,128)(2,1)S(1)} %fusion.29), kind=kOutput, calls=%fused_computation.12 | convolution fusion | flops 10506240 | bytes 5265408 | tf_op jit(solution)/shard_map/bae,oae->bo/dot_general | solution.py:156
  183.4 0.6 gather_fusion.1
  184.0 0.2 bitcast_convert_fusion.3
  184.7 0.8 pad_maximum_fusion
  185.5 1.2 copy.146
  186.7 101.9 %all-reduce.2.cloned.1.call-done = bf16[4,2,5120]{2,1,0:T(2,128)(2,1)} async-done(((bf16[4,2,5120]{2,1,0:T(2,128)(2,1)}), bf16[4,2,5120]{2,1,0:T(2,128)(2,1)}) %all-reduce.2.cloned.1.call-update) | async-done | bytes 81936 | tf_op jit(solution)/shard_map/psum | solution.py:169
  288.6 1.1 multiply_reduce_fusion
  289.7 0.7 fusion.61
  (107 shorter events, 4.9 us)
Async XLA Ops:
  7.2 153.0 %copy-start = (bf16[2,1,2048,128]{3,2,1,0:T(8,128)(2,1)S(1)}, bf16[2,1,2048,128]{3,2,1,0:T(8,128)(2,1)}, u32[]{:S(2)}) copy-start(bf16[2,1,2048,128]{3,2,1,0:T(8,128)(2,1)} %param.24) | copy-start | bytes 3145732
  7.2 138.7 %all-gather.2.cloned.1.call-start = ((), (), s32[]{:S(2)}) async-start(), calls=%async_computation | async-start | bytes 13312000 | tf_op jit(solution)/shard_map/all_gather | solution.py:101
  9.7 278.9 %all-reduce.2.cloned.1.call-start = ((), (), s32[]{:S(2)}) async-start(), calls=%async_computation.1 | async-start | bytes 163840 | tf_op jit(solution)/shard_map/psum | solution.py:169
  145.9 9.9 %copy-start.1 = (bf16[5120,1,1280]{2,0,1:T(8,128)(2,1)S(1)}, bf16[5120,1,1280]{2,0,1:T(8,128)(2,1)}, u32[]{:S(2)}) copy-start(bf16[5120,1,1280]{2,0,1:T(8,128)(2,1)} %all-gather.2.cloned.1.call-done) | copy-start | bytes 39321604
  150.6 12.5 %copy-start.2 = (bf16[2,1,2048,128]{3,2,1,0:T(8,128)(2,1)S(1)}, bf16[2,1,2048,128]{3,2,1,0:T(8,128)(2,1)}, u32[]{:S(2)}) copy-start(bf16[2,1,2048,128]{3,2,1,0:T(8,128)(2,1)} %param.25) | copy-start | bytes 3145732
  163.6 125.0 %copy-start.3 = (bf16[4,2,5120]{2,1,0:T(2,128)(2,1)S(1)}, bf16[4,2,5120]{2,1,0:T(2,128)(2,1)}, u32[]{:S(2)}) copy-start(bf16[4,2,5120]{2,1,0:T(2,128)(2,1)} %param.20) | copy-start | bytes 245764
  163.6 126.1 %copy-start.4 = (f32[640]{0:T(1024)S(1)}, f32[640]{0:T(1024)}, u32[]{:S(2)}) copy-start(f32[640]{0:T(1024)} %param.22) | copy-start | bytes 7684
Sparse Core Ops, SparseCore 0:
  10.7 135.1 all-gather.1
  185.6 102.9 all-reduce.1
where the time goes:
time: 301 us; the launch traced here: 297 us
  waiting for transfers between devices  228 us (76%)
  matrix products  32.4 us (11%)
  between operations  14.5 us (5%)
  other arithmetic  13.3 us (4%)
  local copies, waits for them, and re-layouts  9.39 us (3%)
    all_gather x1, waiting for transfers between devices, body(): gathered = lax.all_gather(fresh_token, ('learn', 'rep'), axis=0, tiled=True)  126 us
    psum x1, waiting for transfers between devices, body(): summed = lax.psum(attn_all.astype(jnp.bfloat16), 'tp').astype(jnp.float32)  102 us
    dot_general x4, matrix products, body(): jnp.einsum('bae,oae->bo', head_split, output_weight_matrix, preferred_ele...  15.8 us
    dot_general x4, matrix products, body(): jnp.einsum('nd,dgc->ngc', stored_order, weights_in, preferred_element_typ...  11.9 us
  transfers between devices with their start and end apart: 2, of which 2 were waited for; matrix products, arithmetic and copies ran while one was open for 4% of the time, Pallas kernels for 0%

commit v1 on v0

v1 whole, which is shorter than its diff:
```python
import functools

import jax
import jax.numpy as jnp
import numpy as np
from jax import lax
from jax.experimental import pallas as pl
from jax.experimental.pallas import tpu as pltpu
from jax.sharding import PartitionSpec as P

MODEL_WIDTH = 5120
HEAD_SIZE = 128
KEY_VALUE_HEADS = 8
QUERY_PER_GROUP = 4
STEPS = 4
CACHE_SLOTS = 2048
BLOCKS = 64
ROWS = 80
IN_COLUMNS = 768
OUT_COLUMNS = 512
TOKENS = 8
QPEERS = 16

beta_one = 0.9
beta_two = 0.95
adam_rate = 0.05
adam_decay = 0.1
adam_epsilon = 1e-08
correction_one = 1.0 - 0.9**10
correction_two = 1.0 - 0.95**10
norm_epsilon = 1e-06
rope_theta = 1000000.0

MESH = pl.DeviceIdType.MESH
F32 = jnp.float32
BF16 = jnp.bfloat16


def adam_update(master, first, second, gradient):
    first_moment = beta_one * first + (1.0 - beta_one) * gradient
    second_moment = beta_two * second + (1.0 - beta_two) * gradient * gradient
    update = (
        first_moment / correction_one / (jnp.sqrt(second_moment / correction_two) + adam_epsilon)
        + adam_decay * master
    )
    return master - adam_rate * update


def widen(block):
    return jnp.concatenate([block, jnp.zeros((block.shape[0], 128 - ROWS), block.dtype)], axis=1)


def kernel(
    order, lengths, x_in, gain_in, post_in, freq_in, master_in, first_in, second_in, gradient_in, keys_in, values_in,
    master_out, mixed_out,
    x_v, gain_v, xs, xblk, hblk, xperm, zblk, master_v, first_v, second_v, gradient_v, keys_v, values_v,
    hs, hr, wq, wo, ps, pr, os, orr, s4, r4, s5, r5,
    load_sem, out_sem, h_send, h_recv, wq_send, wq_recv, ring_send, ring_recv, twin_send, twin_recv,
    p_send, p_recv, o_send, o_recv, r4_send, r4_recv, r5_send, r5_self, r5_recv,
):
    l, r, t = lax.axis_index("learn"), lax.axis_index("rep"), lax.axis_index("tp")
    z, y = lax.div(l, 4), lax.rem(l, 4)
    yp, yy = lax.div(y, 2), lax.rem(y, 2)
    c = z * 2 + yp
    xx, yh = lax.div(t, 2), lax.rem(t, 2)

    def dev(z, y, r, t):
        return {"learn": z * 4 + y, "rep": r, "tp": t}

    def q_peer(d):
        other = lax.rem(c + d, QPEERS)
        return dev(lax.div(other, 2), lax.rem(other, 2) * 2 + yy, r, t)

    twin = dev(z, y, 1 - r, t)
    partner = dev(z, yp * 2 + 1 - yy, r, t)
    diagonal = dev(z, yp * 2 + 1 - yy, 1 - r, t)
    above = dev(lax.rem(z + 1, 8), y, r, t)
    below = dev(lax.rem(z + 7, 8), y, r, t)

    def y_peer(d):
        return dev(z, lax.rem(y + d, 4), r, t)

    def x_peer(e):
        return dev(z, y, r, lax.rem(xx + e, 4) * 2 + yh)

    loads = [
        pltpu.make_async_copy(src, dst, load_sem.at[i])
        for i, (src, dst) in enumerate(
            [
                (x_in, x_v), (gain_in, gain_v), (master_in, master_v), (first_in, first_v), (second_in, second_v),
                (gradient_in, gradient_v), (keys_in, keys_v), (values_in, values_v),
            ]
        )
    ]
    for load in loads:
        load.start()

    barrier = pltpu.get_barrier_semaphore()

    def greet(device):
        pl.semaphore_signal(barrier, inc=1, device_id=device, device_id_type=MESH)

    def greet_q(d, carry):
        greet(q_peer(d))
        return carry

    lax.fori_loop(1, QPEERS, greet_q, 0)
    for device in (twin, partner, diagonal, above, below):
        greet(device)
    for d in range(1, 4):
        greet(y_peer(d))
        greet(x_peer(d))
    for e in range(8):
        there = lax.rem(t + e, 8)
        device = dev(z, lax.rem(y + lax.div(there, 2), 4), r, there)
        if e == 0:
            pl.when(xx != 0)(functools.partial(greet, device))
        else:
            greet(device)
    greetings = (QPEERS - 1) + 5 + 6 + 7 + jnp.where(xx != 0, 1, 0)

    loads[0].wait()
    loads[1].wait()
    for s in range(STEPS):
        xs[2 * s : 2 * s + 2, :] = x_v[s].astype(F32)
    stream = xs[...]
    rscale = lax.rsqrt(jnp.mean(stream * stream, axis=1, keepdims=True) + norm_epsilon)
    for b in range(BLOCKS):
        block = xs[:, b * ROWS : (b + 1) * ROWS]
        xblk[b] = widen(block)
        hblk[b] = widen(block * rscale * gain_v[:, b * ROWS : (b + 1) * ROWS])
    for d in range(QPEERS):
        other = lax.rem(c + d, QPEERS)
        parts = []
        for m in range(4):
            my, mr = m // 2, m % 2
            w = lax.rem(yy + my, 2) * 2 + lax.rem(r + mr, 2)
            parts.append(hblk[order[other * 4 + w]])
        piece = jnp.concatenate(parts, axis=0).astype(BF16)
        if d == 0:
            hr[0] = piece
        else:
            hs[d] = piece

    wq[:, ROWS:, :] = jnp.zeros((4, 128 - ROWS, IN_COLUMNS), BF16)
    for i in range(2, 6):
        loads[i].wait()
    for j in range(10):
        rows = pl.ds(j, ROWS, stride=10)
        fresh = adam_update(
            master_v[rows, :], first_v[rows, :], second_v[rows, :], gradient_v[:, j * 128 : (j + 1) * 128].astype(F32)
        )
        master_v[rows, :] = fresh
        if j < 6:
            wq[0, 0:ROWS, j * 128 : (j + 1) * 128] = fresh.astype(BF16)
        else:
            wo[0, 0, :, (j - 6) * 128 : (j - 5) * 128] = fresh.astype(BF16)
    write_master = pltpu.make_async_copy(master_v, master_out, out_sem)
    write_master.start()

    pl.semaphore_wait(barrier, greetings)

    def send_h(d, carry):
        pltpu.make_async_remote_copy(
            src_ref=hs.at[d], dst_ref=hr.at[d], send_sem=h_send, recv_sem=h_recv, device_id=q_peer(d), device_id_type=MESH
        ).start()
        return carry

    lax.fori_loop(1, QPEERS, send_h, 0)
    for m, device in ((2, partner), (3, diagonal), (1, twin)):
        pltpu.make_async_remote_copy(
            src_ref=wq.at[0, pl.ds(0, ROWS)],
            dst_ref=wq.at[m, pl.ds(0, ROWS)],
            send_sem=wq_send.at[m - 1],
            recv_sem=wq_recv.at[m - 1],
            device_id=device,
            device_id_type=MESH,
        ).start()

    def ring(src, dst, index, device):
        return pltpu.make_async_remote_copy(
            src_ref=wo.at[src, 0],
            dst_ref=wo.at[dst, 0],
            send_sem=ring_send.at[index],
            recv_sem=ring_recv.at[index],
            device_id=device,
            device_id_type=MESH,
        )

    up = [ring(k, k + 1, k, above) for k in range(4)]
    down = [ring((8 - k) % 8, 7 - k, 4 + k, below) for k in range(3)]
    to_twin = [
        pltpu.make_async_remote_copy(
            src_ref=wo.at[k, 0],
            dst_ref=wo.at[k, 1],
            send_sem=twin_send.at[k],
            recv_sem=twin_recv.at[k],
            device_id=twin,
            device_id_type=MESH,
        )
        for k in range(8)
    ]
    up[0].start()
    down[0].start()
    to_twin[0].start()

    token = lax.broadcasted_iota(jnp.int32, (TOKENS, HEAD_SIZE), 0)
    lane = lax.broadcasted_iota(jnp.int32, (TOKENS, HEAD_SIZE), 1)
    positions = jnp.where(lax.rem(token, 2) == 0, lengths[0], lengths[1]) + lax.div(token, 2)
    angles = positions.astype(F32) * freq_in[...]
    cosine = jnp.cos(angles)
    sine = jnp.sin(angles)
    sine = jnp.where(lane < HEAD_SIZE // 2, -sine, sine)

    def find(j, carry):
        actor = order[j] - t * 8
        return tuple(jnp.where(actor == i, j, carry[i]) for i in range(8))

    stored = lax.fori_loop(0, BLOCKS, find, tuple(jnp.int32(0) for _ in range(8)))
    for xs_ in range(4):
        source_y = lax.rem(y + xs_, 4)
        for k in range(8):
            for rr in range(2):
                j = (lax.rem(z + 8 - k, 8) * 4 + source_y) * 2 + lax.rem(r + rr, 2)
                xperm[xs_ * 16 + k * 2 + rr] = xblk[order[j]]

    pltpu.make_async_copy(hr.at[pl.ds(1, QPEERS - 1)], hr.at[pl.ds(1, QPEERS - 1)], h_recv).wait()
    wide = hr[...].astype(F32)
    left = jnp.concatenate([wide[:, 8 * m : 8 * m + 8, :].reshape(QPEERS * TOKENS, 128) for m in range(4)], axis=1).astype(BF16)
    for m in range(3):
        pltpu.make_async_copy(wq.at[0, pl.ds(0, ROWS)], wq.at[0, pl.ds(0, ROWS)], wq_recv.at[m]).wait()
    partial = jnp.dot(left, wq[...].reshape(512, IN_COLUMNS), preferred_element_type=F32).reshape(QPEERS, TOKENS, IN_COLUMNS)
    packed = jnp.concatenate([partial[:, :, :384], partial[:, :, 384:]], axis=1).astype(BF16)
    pr[0] = packed[0]
    ps[...] = packed

    def send_p(d, carry):
        pltpu.make_async_remote_copy(
            src_ref=ps.at[d],
            dst_ref=pr.at[d],
            send_sem=p_send,
            recv_sem=p_recv,
            device_id=q_peer(QPEERS - d),
            device_id_type=MESH,
        ).start()
        return carry

    lax.fori_loop(1, QPEERS, send_p, 0)
    for k in range(1, 4):
        up[k - 1].wait_recv()
        up[k].start()
        to_twin[k].start()
        down[k - 1].wait_recv()
        if k < 3:
            down[k].start()
        to_twin[8 - k].start()
    up[3].wait_recv()
    to_twin[4].start()
    pltpu.make_async_copy(pr.at[pl.ds(1, QPEERS - 1)], pr.at[pl.ds(1, QPEERS - 1)], p_recv).wait()
    projected = jnp.sum(pr[...].astype(F32), axis=0) * np.float32(1.0 / np.sqrt(np.float32(MODEL_WIDTH)))
    top, bottom = projected[0:8], projected[8:16]
    raw = jnp.concatenate(
        [top[:, 0:128], top[:, 128:256], top[:, 256:384], bottom[:, 0:128], bottom[:, 128:256]], axis=0
    )
    new_values = bottom[:, 256:384].astype(BF16)
    normed = raw * lax.rsqrt(jnp.mean(raw * raw, axis=1, keepdims=True) + norm_epsilon)
    cosine5 = jnp.concatenate([cosine] * 5, axis=0)
    sine5 = jnp.concatenate([sine] * 5, axis=0)
    rotated = (normed * cosine5 + pltpu.roll(normed, HEAD_SIZE // 2, 1) * sine5).astype(BF16)
    queries = rotated[0:32]
    new_keys = rotated[32:40]

    scale = HEAD_SIZE ** (-0.5)
    contract_last = (((1,), (1,)), ((), ()))
    loads[6].wait()
    loads[7].wait()
    q_token = lax.rem(lax.broadcasted_iota(jnp.int32, (32, TOKENS), 0), 8)
    k_token = lax.broadcasted_iota(jnp.int32, (32, TOKENS), 1)
    recent = lax.dot_general(queries, new_keys, contract_last, preferred_element_type=F32) * scale
    seen = (lax.rem(q_token, 2) == lax.rem(k_token, 2)) & (lax.div(k_token, 2) <= lax.div(q_token, 2))
    recent = jnp.where(seen, jnp.exp(recent), 0.0)
    total = jnp.sum(recent, axis=1, keepdims=True)
    heads = jnp.dot(recent.astype(BF16), new_values, preferred_element_type=F32)
    slot = lax.broadcasted_iota(jnp.int32, (32, CACHE_SLOTS), 1)
    row_of = lax.rem(lax.broadcasted_iota(jnp.int32, (32, CACHE_SLOTS), 0), 2)
    for n in range(2):
        scores = (
            lax.dot_general(queries, keys_v[n * CACHE_SLOTS : (n + 1) * CACHE_SLOTS, :], contract_last, preferred_element_type=F32)
            * scale
        )
        past = jnp.where((slot < lengths[n]) & (row_of == n), jnp.exp(scores), 0.0)
        total = total + jnp.sum(past, axis=1, keepdims=True)
        heads = heads + jnp.dot(
            past.astype(BF16), values_v[n * CACHE_SLOTS : (n + 1) * CACHE_SLOTS, :], preferred_element_type=F32
        )
    heads = (heads / total).astype(BF16)

    os[...] = heads
    orr[0] = heads
    for d in range(1, 4):
        pltpu.make_async_remote_copy(
            src_ref=os, dst_ref=orr.at[d], send_sem=o_send.at[d - 1], recv_sem=o_recv.at[d - 1], device_id=y_peer(d), device_id_type=MESH
        ).start()
    for k in range(8):
        to_twin[k].wait_recv()
    for d in range(3):
        pltpu.make_async_copy(os, os, o_recv.at[d]).wait()
    wide = orr[...].astype(F32)
    left = jnp.concatenate([wide[:, 8 * h : 8 * h + 8, :].reshape(32, 128) for h in range(4)], axis=1).astype(BF16)
    attn = lax.dot_general(left, wo[...].reshape(16 * ROWS, OUT_COLUMNS), contract_last, preferred_element_type=F32)
    attn = attn * np.float32(1.0 / np.sqrt(np.float32(KEY_VALUE_HEADS * OUT_COLUMNS)))
    attn = attn.reshape(4, 8, 1280)
    s4[...] = jnp.concatenate([attn[:, :, :640], attn[:, :, 640:]], axis=1).astype(BF16)
    for e in range(1, 4):
        pltpu.make_async_remote_copy(
            src_ref=s4.at[lax.rem(xx + e, 4)],
            dst_ref=r4.at[e - 1],
            send_sem=r4_send.at[e - 1],
            recv_sem=r4_recv.at[e - 1],
            device_id=x_peer(e),
            device_id_type=MESH,
        ).start()
    summed = s4[xx].astype(F32)
    for e in range(3):
        pltpu.make_async_copy(s4.at[0], s4.at[0], r4_recv.at[e]).wait()
        summed = summed + r4[e].astype(F32)
    s5[...] = summed.astype(BF16)
    target_y = lax.rem(y + 4 - xx, 4)

    def to_owner(e):
        there = lax.rem(t + e, 8)
        return pltpu.make_async_remote_copy(
            src_ref=s5,
            dst_ref=r5.at[t],
            send_sem=r5_send.at[e],
            recv_sem=r5_recv,
            device_id=dev(z, target_y, r, there),
            device_id_type=MESH,
        )

    def own_copy():
        return pltpu.make_async_copy(s5, r5.at[t], r5_recv)

    for e in range(1, 8):
        to_owner(e).start()

    @pl.when(xx != 0)
    def _():
        to_owner(0).start()

    @pl.when(xx == 0)
    def _():
        own_copy().start()

    pltpu.make_async_copy(r5, r5, r5_recv).wait()

    squares = jnp.zeros((TOKENS, 128), F32)
    for xs_ in range(4):
        both = r5[2 * xs_].astype(F32) + r5[2 * xs_ + 1].astype(F32)
        for b in range(8):
            block = widen(both[:, b * ROWS : (b + 1) * ROWS])
            for half in range(2):
                place = xs_ * 16 + half * 8 + b
                residual = block[half * 8 : half * 8 + 8] + xperm[place]
                zblk[place] = residual
                squares = squares + residual * residual
    rscale = lax.rsqrt(jnp.sum(squares, axis=1, keepdims=True) * np.float32(1.0 / MODEL_WIDTH) + norm_epsilon)
    pieces = []
    for i in range(8):
        j = stored[i]
        k = lax.rem(z + 8 - lax.div(j, 8), 8)
        source = lax.rem(lax.rem(lax.div(j, 2), 4) + 4 - y, 4)
        rr = lax.rem(lax.rem(j, 2) + r, 2)
        pieces.append(zblk[source * 16 + k * 2 + rr][:, :ROWS])
    mixed_out[...] = (jnp.concatenate(pieces, axis=1) * rscale * post_in[...]).astype(BF16)

    write_master.wait()
    pltpu.make_async_copy(hs.at[pl.ds(1, QPEERS - 1)], hs.at[pl.ds(1, QPEERS - 1)], h_send).wait()
    pltpu.make_async_copy(ps.at[pl.ds(1, QPEERS - 1)], ps.at[pl.ds(1, QPEERS - 1)], p_send).wait()
    for m in range(3):
        pltpu.make_async_copy(wq.at[0, pl.ds(0, ROWS)], wq.at[0, pl.ds(0, ROWS)], wq_send.at[m]).wait()
    for copy in up + down + to_twin:
        copy.wait_send()
    for d in range(3):
        pltpu.make_async_copy(os, os, o_send.at[d]).wait()
        pltpu.make_async_copy(s4.at[0], s4.at[0], r4_send.at[d]).wait()
    for e in range(1, 8):
        to_owner(e).wait_send()

    @pl.when(xx != 0)
    def _():
        to_owner(0).wait_send()


def body(
    master, adam_first_moment, adam_second_moment, gradient, resync_order, inputs, in_gain, post_gain, lengths,
    cached_key_rows, cached_value_rows,
):
    half = np.arange(HEAD_SIZE // 2, dtype=np.float64)
    freqs = (rope_theta ** (-(half * 2.0 / HEAD_SIZE))).astype(np.float32)
    freqs = jnp.asarray(np.concatenate([freqs, freqs])[None, :])
    smem = pl.BlockSpec(memory_space=pltpu.SMEM)
    vmem = pl.BlockSpec(memory_space=pltpu.VMEM)
    anywhere = pl.BlockSpec(memory_space=pl.ANY)
    dma = pltpu.SemaphoreType.DMA
    flat = (ROWS * 10, 128)
    new_master, mixed = pl.pallas_call(
        kernel,
        out_shape=(jax.ShapeDtypeStruct(flat, F32), jax.ShapeDtypeStruct((TOKENS, 640), BF16)),
        in_specs=[smem, smem, anywhere, anywhere, vmem, vmem] + [anywhere] * 6,
        out_specs=(anywhere, vmem),
        scratch_shapes=[
            pltpu.VMEM((STEPS, 2, MODEL_WIDTH), BF16),
            pltpu.VMEM((1, MODEL_WIDTH), F32),
            pltpu.VMEM((TOKENS, MODEL_WIDTH), F32),
            pltpu.VMEM((BLOCKS, TOKENS, 128), F32),
            pltpu.VMEM((BLOCKS, TOKENS, 128), F32),
            pltpu.VMEM((BLOCKS, TOKENS, 128), F32),
            pltpu.VMEM((BLOCKS, TOKENS, 128), F32),
            pltpu.VMEM(flat, F32),
            pltpu.VMEM(flat, F32),
            pltpu.VMEM(flat, F32),
            pltpu.VMEM((ROWS, 1280), BF16),
            pltpu.VMEM((2 * CACHE_SLOTS, HEAD_SIZE), BF16),
            pltpu.VMEM((2 * CACHE_SLOTS, HEAD_SIZE), BF16),
            pltpu.VMEM((QPEERS, 32, 128), BF16),
            pltpu.VMEM((QPEERS, 32, 128), BF16),
            pltpu.VMEM((4, 128, IN_COLUMNS), BF16),
            pltpu.VMEM((8, 2, ROWS, OUT_COLUMNS), BF16),
            pltpu.VMEM((QPEERS, 16, 384), BF16),
            pltpu.VMEM((QPEERS, 16, 384), BF16),
            pltpu.VMEM((32, 128), BF16),
            pltpu.VMEM((4, 32, 128), BF16),
            pltpu.VMEM((4, 16, 640), BF16),
            pltpu.VMEM((3, 16, 640), BF16),
            pltpu.VMEM((16, 640), BF16),
            pltpu.VMEM((8, 16, 640), BF16),
            dma((8,)), dma, dma, dma, dma((3,)), dma((3,)), dma((7,)), dma((7,)), dma((8,)), dma((8,)),
            dma, dma, dma((3,)), dma((3,)), dma((3,)), dma((3,)), dma((8,)), dma, dma,
        ],
        compiler_params=pltpu.CompilerParams(collective_id=0, has_side_effects=True, vmem_limit_bytes=40 << 20),
        cost_estimate=pl.CostEstimate(flops=400_000_000, bytes_accessed=4_500_000, transcendentals=200_000),
        name="adam_attention",
    )(
        resync_order, lengths, inputs, in_gain.reshape(1, MODEL_WIDTH), post_gain.reshape(1, 640), freqs,
        master.reshape(flat), adam_first_moment.reshape(flat), adam_second_moment.reshape(flat), gradient.reshape(ROWS, 1280),
        cached_key_rows.reshape(2 * CACHE_SLOTS, HEAD_SIZE), cached_value_rows.reshape(2 * CACHE_SLOTS, HEAD_SIZE),
    )
    return new_master.reshape(ROWS, 1, 1280), mixed.reshape(STEPS, 2, 640)


def solution(mesh):
    in_specs = (
        P(("learn", "rep"), "tp", None),
        P(("learn", "rep"), "tp", None),
        P(("learn", "rep"), "tp", None),
        P(("learn", "rep"), "tp", None),
        P(),
        P(None, ("learn", "rep"), None),
        P(),
        P("tp"),
        P(("learn", "rep")),
        P(("learn", "rep"), "tp", None, None),
        P(("learn", "rep"), "tp", None, None),
    )
    out_specs = (P(("learn", "rep"), "tp", None), P(None, ("learn", "rep"), "tp"))
    return jax.shard_map(body, mesh=mesh, in_specs=in_specs, out_specs=out_specs, check_vma=False)
```

time: 301 us -> 67.8 us (0.23)
  waiting for transfers between devices: 228 us -> 0 us
  Pallas kernels: 0 us -> 55.6 us
  matrix products: 32.4 us -> 0 us
  between operations: 14.5 us -> 0.66 us
  other arithmetic: 13.3 us -> 0 us
    all_gather x1 -> x0, waiting for transfers between devices: 126 us -> none  [body(): gathered = lax.all_gather(fresh_token, ('learn', 'rep'), axis=0, tiled=True)]
    psum x1 -> x0, waiting for transfers between devices: 102 us -> none  [body(): summed = lax.psum(attn_all.astype(jnp.bfloat16), 'tp').astype(jnp.float32)]
    pallas_call x0 -> x1, Pallas kernels: none -> 55.6 us  [body(): pl.pallas_call(kernel, out_shape=(jax.ShapeDtypeStruct(flat, F32), jax.Sh...]
    dot_general x23 -> x0, matrix products: 32.4 us -> none  [the longest x4 15.8 us: body(): jnp.einsum('bae,oae->bo', head_split, output_weight_matrix, preferred_ele...]
    unnamed x11 -> x25, local copies, waits for them, and re-layouts: 1.2 us -> 10.1 us
    gather x8 -> x0, local copies, waits for them, and re-layouts: 5.15 us -> none  [the longest x4 2.58 us: body(): jnp.take(normed_in.reshape(count_of_rows, shards, row_block), resync_orde...]
    convert_element_type x5 -> x0, other arithmetic: 4.81 us -> none  [the longest x1 2.44 us: body(): fresh_token = new_master.astype(jnp.bfloat16)]
    reduce_sum x11 -> x0, other arithmetic: 3.71 us -> none  [the longest x1 1.11 us: body(): jnp.mean(residual * residual, axis=2, keepdims=True) + norm_epsilon]
  transfers between devices with their start and end apart: 2 -> 0, of which waited for: 2 -> 0; matrix products, arithmetic and copies ran while one was open for 4% -> 0% of each run, Pallas kernels for 0% -> 0%
where the time goes in v1:
time: 67.8 us; the launch traced here: 67 us
  Pallas kernels  55.6 us (82%)
  local copies, waits for them, and re-layouts  10.7 us (16%)
    pallas_call x1, Pallas kernels, body(): pl.pallas_call(kernel, out_shape=(jax.ShapeDtypeStruct(flat, F32), jax.Sh...  55.6 us
    unnamed x25, local copies, waits for them, and re-layouts  10.1 us

profile of v1, /device:TPU:6, one launch (start us, length us, event | category | flops | bytes accessed | tf_op | source)
XLA Modules:
  0.0 67.0 jit_solution(8381922079067270243)
XLA Ops:
  0.6 0.0 copy-start.11
  0.6 0.7 %copy-done.11 = f32[640]{0:T(1024)S(1)} copy-done((f32[640]{0:T(1024)S(1)}, f32[640]{0:T(1024)}, u32[]{:S(2)}) %copy-start.11) | copy-done | bytes 2584
  1.3 0.0 copy-start.8
  1.3 0.0 copy-start.9
  1.3 0.0 copy-start.10
  1.3 0.6 copy-done.8
  2.0 0.0 copy-done.9
  2.0 0.0 copy-done.10
  2.0 0.0 copy-start
  2.0 1.2 %copy-done = bf16[2,1,2048,128]{3,2,1,0:T(8,128)(2,1)S(1)} copy-done((bf16[2,1,2048,128]{3,2,1,0:T(8,128)(2,1)S(1)}, bf16[2,1,2048,128]{3,2,1,0:T(8,128)(2,1)}, u32[]{:S(2)}) %copy-start) | copy-done | bytes 1048600
  3.2 0.0 copy-start.1
  3.2 1.2 %copy-done.1 = bf16[2,1,2048,128]{3,2,1,0:T(8,128)(2,1)S(1)} copy-done((bf16[2,1,2048,128]{3,2,1,0:T(8,128)(2,1)S(1)}, bf16[2,1,2048,128]{3,2,1,0:T(8,128)(2,1)}, u32[]{:S(2)}) %copy-start.1) | copy-done | bytes 1048600
  4.5 0.0 copy-start.2
  4.5 1.0 %copy-done.2 = f32[80,1,1280]{2,1,0:T(1,128)S(1)} copy-done((f32[80,1,1280]{2,1,0:T(1,128)S(1)}, f32[80,1,1280]{2,1,0:T(1,128)}, u32[]{:S(2)}) %copy-start.2) | copy-done | bytes 409624
  5.5 0.0 copy-start.3
  5.5 1.0 %copy-done.3 = f32[80,1,1280]{2,1,0:T(1,128)S(1)} copy-done((f32[80,1,1280]{2,1,0:T(1,128)S(1)}, f32[80,1,1280]{2,1,0:T(1,128)}, u32[]{:S(2)}) %copy-start.3) | copy-done | bytes 409624
  6.5 0.0 copy-start.4
  6.5 1.0 %copy-done.4 = f32[80,1,1280]{2,1,0:T(1,128)S(1)} copy-done((f32[80,1,1280]{2,1,0:T(1,128)S(1)}, f32[80,1,1280]{2,1,0:T(1,128)}, u32[]{:S(2)}) %copy-start.4) | copy-done | bytes 409624
  7.5 0.0 copy-start.5
  7.5 0.9 %copy-done.5 = bf16[80,1,1280]{2,0,1:T(8,128)(2,1)S(1)} copy-done((bf16[80,1,1280]{2,0,1:T(8,128)(2,1)S(1)}, bf16[80,1,1280]{2,0,1:T(8,128)(2,1)}, u32[]{:S(2)}) %copy-start.5) | copy-done | bytes 204824
  8.4 0.0 copy-start.6
  8.4 0.9 %copy-done.6 = bf16[4,2,5120]{2,1,0:T(2,128)(2,1)S(1)} copy-done((bf16[4,2,5120]{2,1,0:T(2,128)(2,1)S(1)}, bf16[4,2,5120]{2,1,0:T(2,128)(2,1)}, u32[]{:S(2)}) %copy-start.6) | copy-done | bytes 81944
  9.3 0.0 copy-start.7
  9.3 0.7 %copy-done.7 = f32[5120]{0:T(1024)S(1)} copy-done((f32[5120]{0:T(1024)S(1)}, f32[5120]{0:T(1024)}, u32[]{:S(2)}) %copy-start.7) | copy-done | bytes 20504
  10.0 55.6 %adam_attention.1 = (f32[800,128]{1,0:T(8,128)S(1)}, bf16[8,640]{1,0:T(8,128)(2,1)S(1)}) custom-call(s32[64]{0:T(128)S(1)} %copy-done.8, s32[2]{0:T(128)S(1)} %copy-done.9, bf16[4,2,5120]{2,1,0:T(2,128)(2,1)S(1)} %copy-done.6, f32[1,5120]{1,0:T(1,128)S(1)} %bitcast.15, f32[1,640]{1,0:T(1,128)S(1)} %reshape.35.post_in, f32[1,128]{1,0:T(1,128)S(1)} %copy-done.10, ...), custom_call_target="tpu_custom_call" | custom-call | flops 400000000 | bytes 4500000 | tf_op jit(solution)/shard_map/adam_attention/pallas_call | solution.py:407
  65.6 0.6 reshape.43
  66.2 0.8 %copy.16 = f32[80,1,1280]{2,1,0:T(1,128)} copy(f32[80,1,1280]{2,1,0:T(1,128)S(1)} %bitcast.13) | data formatting | bytes 819200
  (1 shorter events, 0.0 us)
Async XLA Ops:
  0.6 0.7 %copy-start.11 = (f32[640]{0:T(1024)S(1)}, f32[640]{0:T(1024)}, u32[]{:S(2)}) copy-start(f32[640]{0:T(1024)} %param.19) | copy-start | bytes 7684
  1.3 0.7 copy-start.8
  1.3 0.7 copy-start.9
  1.3 0.7 %copy-start.10 = (f32[1,128]{1,0:T(1,128)S(1)}, f32[1,128]{1,0:T(1,128)}, u32[]{:S(2)}) copy-start(f32[1,128]{1,0:T(1,128)} %constant.2.clone.freq_in) | copy-start | bytes 1540
  2.0 1.2 %copy-start = (bf16[2,1,2048,128]{3,2,1,0:T(8,128)(2,1)S(1)}, bf16[2,1,2048,128]{3,2,1,0:T(8,128)(2,1)}, u32[]{:S(2)}) copy-start(bf16[2,1,2048,128]{3,2,1,0:T(8,128)(2,1)} %param.21) | copy-start | bytes 3145732
  3.2 1.2 %copy-start.1 = (bf16[2,1,2048,128]{3,2,1,0:T(8,128)(2,1)S(1)}, bf16[2,1,2048,128]{3,2,1,0:T(8,128)(2,1)}, u32[]{:S(2)}) copy-start(bf16[2,1,2048,128]{3,2,1,0:T(8,128)(2,1)} %param.22) | copy-start | bytes 3145732
  4.5 1.0 %copy-start.2 = (f32[80,1,1280]{2,1,0:T(1,128)S(1)}, f32[80,1,1280]{2,1,0:T(1,128)}, u32[]{:S(2)}) copy-start(f32[80,1,1280]{2,1,0:T(1,128)} %param.12) | copy-start | bytes 1228804
  5.5 1.0 %copy-start.3 = (f32[80,1,1280]{2,1,0:T(1,128)S(1)}, f32[80,1,1280]{2,1,0:T(1,128)}, u32[]{:S(2)}) copy-start(f32[80,1,1280]{2,1,0:T(1,128)} %param.13) | copy-start | bytes 1228804
  6.5 1.0 %copy-start.4 = (f32[80,1,1280]{2,1,0:T(1,128)S(1)}, f32[80,1,1280]{2,1,0:T(1,128)}, u32[]{:S(2)}) copy-start(f32[80,1,1280]{2,1,0:T(1,128)} %param.14) | copy-start | bytes 1228804
  7.5 0.9 %copy-start.5 = (bf16[80,1,1280]{2,0,1:T(8,128)(2,1)S(1)}, bf16[80,1,1280]{2,0,1:T(8,128)(2,1)}, u32[]{:S(2)}) copy-start(bf16[80,1,1280]{2,0,1:T(8,128)(2,1)} %param.15) | copy-start | bytes 614404
  8.4 0.9 %copy-start.6 = (bf16[4,2,5120]{2,1,0:T(2,128)(2,1)S(1)}, bf16[4,2,5120]{2,1,0:T(2,128)(2,1)}, u32[]{:S(2)}) copy-start(bf16[4,2,5120]{2,1,0:T(2,128)(2,1)} %x_in.1) | copy-start | bytes 245764
  9.3 0.7 %copy-start.7 = (f32[5120]{0:T(1024)S(1)}, f32[5120]{0:T(1024)}, u32[]{:S(2)}) copy-start(f32[5120]{0:T(1024)} %param.18) | copy-start | bytes 61444

commit v2 on v1

--- a/solution.py
+++ b/solution.py
@@ -51,9 +51,9 @@
 
 
 def kernel(
-    order, lengths, x_in, gain_in, post_in, freq_in, master_in, first_in, second_in, gradient_in, keys_in, values_in,
+    order_in, lengths_in, x_in, gain_in, post_in, freq_in, master_in, first_in, second_in, gradient_in, keys_in, values_in,
     master_out, mixed_out,
-    x_v, gain_v, xs, xblk, hblk, xperm, zblk, master_v, first_v, second_v, gradient_v, keys_v, values_v,
+    order, lengths, post_v, freq_v, x_v, gain_v, xs, xblk, hblk, xperm, zblk, master_v, first_v, second_v, gradient_v, keys_v, values_v,
     hs, hr, wq, wo, ps, pr, os, orr, s4, r4, s5, r5,
     load_sem, out_sem, h_send, h_recv, wq_send, wq_recv, ring_send, ring_recv, twin_send, twin_recv,
     p_send, p_recv, o_send, o_recv, r4_send, r4_recv, r5_send, r5_self, r5_recv,
@@ -83,12 +83,15 @@
     def x_peer(e):
         return dev(z, y, r, lax.rem(xx + e, 4) * 2 + yh)
 
+    pending = []
+
     loads = [
         pltpu.make_async_copy(src, dst, load_sem.at[i])
         for i, (src, dst) in enumerate(
             [
                 (x_in, x_v), (gain_in, gain_v), (master_in, master_v), (first_in, first_v), (second_in, second_v),
                 (gradient_in, gradient_v), (keys_in, keys_v), (values_in, values_v),
+                (order_in, order), (lengths_in, lengths), (post_in, post_v), (freq_in, freq_v),
             ]
         )
     ]
@@ -121,6 +124,7 @@
 
     loads[0].wait()
     loads[1].wait()
+    loads[8].wait()
     for s in range(STEPS):
         xs[2 * s : 2 * s + 2, :] = x_v[s].astype(F32)
     stream = xs[...]
@@ -157,6 +161,7 @@
             wo[0, 0, :, (j - 6) * 128 : (j - 5) * 128] = fresh.astype(BF16)
     write_master = pltpu.make_async_copy(master_v, master_out, out_sem)
     write_master.start()
+    pending.append(write_master.wait)
 
     pl.semaphore_wait(barrier, greetings)
 
@@ -167,15 +172,18 @@
         return carry
 
     lax.fori_loop(1, QPEERS, send_h, 0)
+    pending.append(pltpu.make_async_copy(hs.at[pl.ds(1, QPEERS - 1)], hs.at[pl.ds(1, QPEERS - 1)], h_send).wait)
     for m, device in ((2, partner), (3, diagonal), (1, twin)):
-        pltpu.make_async_remote_copy(
+        copy = pltpu.make_async_remote_copy(
             src_ref=wq.at[0, pl.ds(0, ROWS)],
             dst_ref=wq.at[m, pl.ds(0, ROWS)],
             send_sem=wq_send.at[m - 1],
             recv_sem=wq_recv.at[m - 1],
             device_id=device,
             device_id_type=MESH,
-        ).start()
+        )
+        copy.start()
+        pending.append(copy.wait_send)
 
     def ring(src, dst, index, device):
         return pltpu.make_async_remote_copy(
@@ -200,14 +208,18 @@
         )
         for k in range(8)
     ]
+    pending.extend(copy.wait_send for copy in up + down + to_twin)
     up[0].start()
     down[0].start()
     to_twin[0].start()
 
+    loads[9].wait()
+    loads[10].wait()
+    loads[11].wait()
     token = lax.broadcasted_iota(jnp.int32, (TOKENS, HEAD_SIZE), 0)
     lane = lax.broadcasted_iota(jnp.int32, (TOKENS, HEAD_SIZE), 1)
     positions = jnp.where(lax.rem(token, 2) == 0, lengths[0], lengths[1]) + lax.div(token, 2)
-    angles = positions.astype(F32) * freq_in[...]
+    angles = positions.astype(F32) * freq_v[...]
     cosine = jnp.cos(angles)
     sine = jnp.sin(angles)
     sine = jnp.where(lane < HEAD_SIZE // 2, -sine, sine)
@@ -246,6 +258,7 @@
         return carry
 
     lax.fori_loop(1, QPEERS, send_p, 0)
+    pending.append(pltpu.make_async_copy(ps.at[pl.ds(1, QPEERS - 1)], ps.at[pl.ds(1, QPEERS - 1)], p_send).wait)
     for k in range(1, 4):
         up[k - 1].wait_recv()
         up[k].start()
@@ -298,9 +311,11 @@
     os[...] = heads
     orr[0] = heads
     for d in range(1, 4):
-        pltpu.make_async_remote_copy(
+        copy = pltpu.make_async_remote_copy(
             src_ref=os, dst_ref=orr.at[d], send_sem=o_send.at[d - 1], recv_sem=o_recv.at[d - 1], device_id=y_peer(d), device_id_type=MESH
-        ).start()
+        )
+        copy.start()
+        pending.append(copy.wait_send)
     for k in range(8):
         to_twin[k].wait_recv()
     for d in range(3):
@@ -312,14 +327,16 @@
     attn = attn.reshape(4, 8, 1280)
     s4[...] = jnp.concatenate([attn[:, :, :640], attn[:, :, 640:]], axis=1).astype(BF16)
     for e in range(1, 4):
-        pltpu.make_async_remote_copy(
+        copy = pltpu.make_async_remote_copy(
             src_ref=s4.at[lax.rem(xx + e, 4)],
             dst_ref=r4.at[e - 1],
             send_sem=r4_send.at[e - 1],
             recv_sem=r4_recv.at[e - 1],
             device_id=x_peer(e),
             device_id_type=MESH,
-        ).start()
+        )
+        copy.start()
+        pending.append(copy.wait_send)
     summed = s4[xx].astype(F32)
     for e in range(3):
         pltpu.make_async_copy(s4.at[0], s4.at[0], r4_recv.at[e]).wait()
@@ -343,6 +360,8 @@
 
     for e in range(1, 8):
         to_owner(e).start()
+        pending.append(to_owner(e).wait_send)
+    pending.append(lambda: pl.when(xx != 0)(to_owner(0).wait_send))
 
     @pl.when(xx != 0)
     def _():
@@ -372,24 +391,10 @@
         source = lax.rem(lax.rem(lax.div(j, 2), 4) + 4 - y, 4)
         rr = lax.rem(lax.rem(j, 2) + r, 2)
         pieces.append(zblk[source * 16 + k * 2 + rr][:, :ROWS])
-    mixed_out[...] = (jnp.concatenate(pieces, axis=1) * rscale * post_in[...]).astype(BF16)
-
-    write_master.wait()
-    pltpu.make_async_copy(hs.at[pl.ds(1, QPEERS - 1)], hs.at[pl.ds(1, QPEERS - 1)], h_send).wait()
-    pltpu.make_async_copy(ps.at[pl.ds(1, QPEERS - 1)], ps.at[pl.ds(1, QPEERS - 1)], p_send).wait()
-    for m in range(3):
-        pltpu.make_async_copy(wq.at[0, pl.ds(0, ROWS)], wq.at[0, pl.ds(0, ROWS)], wq_send.at[m]).wait()
-    for copy in up + down + to_twin:
-        copy.wait_send()
-    for d in range(3):
-        pltpu.make_async_copy(os, os, o_send.at[d]).wait()
-        pltpu.make_async_copy(s4.at[0], s4.at[0], r4_send.at[d]).wait()
-    for e in range(1, 8):
-        to_owner(e).wait_send()
-
-    @pl.when(xx != 0)
-    def _():
-        to_owner(0).wait_send()
+    mixed_out[...] = (jnp.concatenate(pieces, axis=1) * rscale * post_v[...].reshape(1, 640)).astype(BF16)
+
+    for wait in pending:
+        wait()
 
 
 def body(
@@ -399,17 +404,20 @@
     half = np.arange(HEAD_SIZE // 2, dtype=np.float64)
     freqs = (rope_theta ** (-(half * 2.0 / HEAD_SIZE))).astype(np.float32)
     freqs = jnp.asarray(np.concatenate([freqs, freqs])[None, :])
-    smem = pl.BlockSpec(memory_space=pltpu.SMEM)
     vmem = pl.BlockSpec(memory_space=pltpu.VMEM)
-    anywhere = pl.BlockSpec(memory_space=pl.ANY)
+    hbm = pl.BlockSpec(memory_space=pltpu.HBM)
     dma = pltpu.SemaphoreType.DMA
     flat = (ROWS * 10, 128)
     new_master, mixed = pl.pallas_call(
         kernel,
         out_shape=(jax.ShapeDtypeStruct(flat, F32), jax.ShapeDtypeStruct((TOKENS, 640), BF16)),
-        in_specs=[smem, smem, anywhere, anywhere, vmem, vmem] + [anywhere] * 6,
-        out_specs=(anywhere, vmem),
+        in_specs=[hbm] * 12,
+        out_specs=(hbm, vmem),
         scratch_shapes=[
+            pltpu.SMEM((BLOCKS,), jnp.int32),
+            pltpu.SMEM((2,), jnp.int32),
+            pltpu.VMEM((640,), F32),
+            pltpu.VMEM((1, HEAD_SIZE), F32),
             pltpu.VMEM((STEPS, 2, MODEL_WIDTH), BF16),
             pltpu.VMEM((1, MODEL_WIDTH), F32),
             pltpu.VMEM((TOKENS, MODEL_WIDTH), F32),
@@ -435,14 +443,14 @@
             pltpu.VMEM((3, 16, 640), BF16),
             pltpu.VMEM((16, 640), BF16),
             pltpu.VMEM((8, 16, 640), BF16),
-            dma((8,)), dma, dma, dma, dma((3,)), dma((3,)), dma((7,)), dma((7,)), dma((8,)), dma((8,)),
+            dma((12,)), dma, dma, dma, dma((3,)), dma((3,)), dma((7,)), dma((7,)), dma((8,)), dma((8,)),
             dma, dma, dma((3,)), dma((3,)), dma((3,)), dma((3,)), dma((8,)), dma, dma,
         ],
-        compiler_params=pltpu.CompilerParams(collective_id=0, has_side_effects=True, vmem_limit_bytes=40 << 20),
+        compiler_params=pltpu.CompilerParams(collective_id=0, has_side_effects=True, vmem_limit_bytes=56 << 20),
         cost_estimate=pl.CostEstimate(flops=400_000_000, bytes_accessed=4_500_000, transcendentals=200_000),
         name="adam_attention",
     )(
-        resync_order, lengths, inputs, in_gain.reshape(1, MODEL_WIDTH), post_gain.reshape(1, 640), freqs,
+        resync_order, lengths, inputs, in_gain.reshape(1, MODEL_WIDTH), post_gain, freqs,
         master.reshape(flat), adam_first_moment.reshape(flat), adam_second_moment.reshape(flat), gradient.reshape(ROWS, 1280),
         cached_key_rows.reshape(2 * CACHE_SLOTS, HEAD_SIZE), cached_value_rows.reshape(2 * CACHE_SLOTS, HEAD_SIZE),
     )

time: 67.8 us -> 58.9 us (0.87)
  local copies, waits for them, and re-layouts: 10.7 us -> 3.11 us
  Pallas kernels: 55.6 us -> 54.5 us
    unnamed x25 -> x1, local copies, waits for them, and re-layouts: 10.1 us -> 1.8 us
    pallas_call x1, Pallas kernels: 55.6 us -> 54.5 us  [body(): pl.pallas_call(kernel, out_shape=(jax.ShapeDtypeStruct(flat, F32), jax.Sh...]
    reshape x1, local copies, waits for them, and re-layouts: 0.61 us -> 1.31 us  [body(): return (new_master.reshape(ROWS, 1, 1280), mixed.reshape(STEPS, 2, 640))]
where the time goes in v2:
time: 58.9 us; the launch traced here: 58.3 us
  Pallas kernels  54.5 us (93%)
  local copies, waits for them, and re-layouts  3.11 us (5%)
  between operations  0.64 us (1%)
    pallas_call x1, Pallas kernels, body(): pl.pallas_call(kernel, out_shape=(jax.ShapeDtypeStruct(flat, F32), jax.Sh...  54.5 us
    unnamed x1, local copies, waits for them, and re-layouts  1.8 us
    reshape x1, local copies, waits for them, and re-layouts, body(): return (new_master.reshape(ROWS, 1, 1280), mixed.reshape(STEPS, 2, 640))  1.31 us

profile of v2, /device:TPU:6, one launch (start us, length us, event | category | flops | bytes accessed | tf_op | source)
XLA Modules:
  0.0 58.3 jit_solution(11071064996816697871)
XLA Ops:
  0.6 54.5 %adam_attention.1 = (f32[800,128]{1,0:T(8,128)}, bf16[8,640]{1,0:T(8,128)(2,1)}) custom-call(s32[64]{0:T(128)} %order_in.1, s32[2]{0:T(128)} %lengths_in.1, bf16[4,2,5120]{2,1,0:T(2,128)(2,1)} %x_in.1, f32[1,5120]{1,0:T(1,128)} %bitcast.15, f32[640]{0:T(1024)} %post_in.1, f32[1,128]{1,0:T(1,128)} %constant.2.clone.freq_in, f32[800,128]{1,0:T(8,128)} %bitcast.11, ...), custom_call_target="tpu_custom_call" | custom-call | flops 400000000 | bytes 4500000 | tf_op jit(solution)/shard_map/adam_attention/pallas_call | solution.py:411
  55.2 1.3 %reshape.39 = bf16[4,2,640]{2,1,0:T(2,128)(2,1)} reshape(bf16[8,640]{1,0:T(8,128)(2,1)} %get-tuple-element.5) | data formatting | bytes 20480 | tf_op jit(solution)/shard_map/reshape | solution.py:457
  56.5 1.8 %copy.16 = f32[80,1,1280]{2,1,0:T(1,128)} copy(f32[80,1,1280]{2,1,0:T(1,128)} %bitcast.10) | data formatting | bytes 819200

commit v3 on v2

--- a/solution.py
+++ b/solution.py
@@ -53,9 +53,9 @@
 def kernel(
     order_in, lengths_in, x_in, gain_in, post_in, freq_in, master_in, first_in, second_in, gradient_in, keys_in, values_in,
     master_out, mixed_out,
-    order, lengths, post_v, freq_v, x_v, gain_v, xs, xblk, hblk, xperm, zblk, master_v, first_v, second_v, gradient_v, keys_v, values_v,
+    order, lengths, post_v, freq_v, x_v, gain_v, xs, qh, hh, xblk, hblk, xperm, zblk, master_v, first_v, second_v, gradient_v, keys_v, values_v,
     hs, hr, wq, wo, ps, pr, os, orr, s4, r4, s5, r5,
-    load_sem, out_sem, h_send, h_recv, wq_send, wq_recv, ring_send, ring_recv, twin_send, twin_recv,
+    load_sem, h_send, h_recv, wq_send, wq_recv, ring_send, ring_recv, twin_send, twin_recv,
     p_send, p_recv, o_send, o_recv, r4_send, r4_recv, r5_send, r5_self, r5_recv,
 ):
     l, r, t = lax.axis_index("learn"), lax.axis_index("rep"), lax.axis_index("tp")
@@ -73,7 +73,6 @@
 
     twin = dev(z, y, 1 - r, t)
     partner = dev(z, yp * 2 + 1 - yy, r, t)
-    diagonal = dev(z, yp * 2 + 1 - yy, 1 - r, t)
     above = dev(lax.rem(z + 1, 8), y, r, t)
     below = dev(lax.rem(z + 7, 8), y, r, t)
 
@@ -108,7 +107,7 @@
         return carry
 
     lax.fori_loop(1, QPEERS, greet_q, 0)
-    for device in (twin, partner, diagonal, above, below):
+    for device in (twin, partner, above, below):
         greet(device)
     for d in range(1, 4):
         greet(y_peer(d))
@@ -120,7 +119,7 @@
             pl.when(xx != 0)(functools.partial(greet, device))
         else:
             greet(device)
-    greetings = (QPEERS - 1) + 5 + 6 + 7 + jnp.where(xx != 0, 1, 0)
+    greetings = (QPEERS - 1) + 4 + 6 + 7 + jnp.where(xx != 0, 1, 0)
 
     loads[0].wait()
     loads[1].wait()
@@ -154,36 +153,41 @@
         fresh = adam_update(
             master_v[rows, :], first_v[rows, :], second_v[rows, :], gradient_v[:, j * 128 : (j + 1) * 128].astype(F32)
         )
-        master_v[rows, :] = fresh
+        master_out[rows, :] = fresh
         if j < 6:
             wq[0, 0:ROWS, j * 128 : (j + 1) * 128] = fresh.astype(BF16)
         else:
             wo[0, 0, :, (j - 6) * 128 : (j - 5) * 128] = fresh.astype(BF16)
-    write_master = pltpu.make_async_copy(master_v, master_out, out_sem)
-    write_master.start()
-    pending.append(write_master.wait)
 
     pl.semaphore_wait(barrier, greetings)
 
-    def send_h(d, carry):
+    def far_first(i):
+        return QPEERS // 2 + jnp.where(lax.rem(i, 2) == 1, lax.div(i + 1, 2), -lax.div(i, 2))
+
+    def send_h(i, carry):
+        d = far_first(i)
         pltpu.make_async_remote_copy(
             src_ref=hs.at[d], dst_ref=hr.at[d], send_sem=h_send, recv_sem=h_recv, device_id=q_peer(d), device_id_type=MESH
         ).start()
         return carry
 
-    lax.fori_loop(1, QPEERS, send_h, 0)
+    lax.fori_loop(0, QPEERS - 1, send_h, 0)
     pending.append(pltpu.make_async_copy(hs.at[pl.ds(1, QPEERS - 1)], hs.at[pl.ds(1, QPEERS - 1)], h_send).wait)
-    for m, device in ((2, partner), (3, diagonal), (1, twin)):
-        copy = pltpu.make_async_remote_copy(
-            src_ref=wq.at[0, pl.ds(0, ROWS)],
-            dst_ref=wq.at[m, pl.ds(0, ROWS)],
-            send_sem=wq_send.at[m - 1],
-            recv_sem=wq_recv.at[m - 1],
+
+    def share(src, dst, device):
+        return pltpu.make_async_remote_copy(
+            src_ref=wq.at[src, pl.ds(0, ROWS)],
+            dst_ref=wq.at[dst, pl.ds(0, ROWS)],
+            send_sem=wq_send.at[dst - 1],
+            recv_sem=wq_recv.at[dst - 1],
             device_id=device,
             device_id_type=MESH,
         )
-        copy.start()
-        pending.append(copy.wait_send)
+
+    shares = [share(0, 1, twin), share(0, 2, partner), share(2, 3, twin)]
+    pending.extend(copy.wait_send for copy in shares)
+    shares[1].start()
+    shares[0].start()
 
     def ring(src, dst, index, device):
         return pltpu.make_async_remote_copy(
@@ -209,6 +213,20 @@
         for k in range(8)
     ]
     pending.extend(copy.wait_send for copy in up + down + to_twin)
+    ring_step = [0]
+
+    def ring_advance():
+        ring_step[0] += 1
+        k = ring_step[0]
+        up[k - 1].wait_recv()
+        if k < 4:
+            up[k].start()
+            down[k - 1].wait_recv()
+            if k < 3:
+                down[k].start()
+            to_twin[8 - k].start()
+        to_twin[k].start()
+
     up[0].start()
     down[0].start()
     to_twin[0].start()
@@ -236,17 +254,22 @@
                 j = (lax.rem(z + 8 - k, 8) * 4 + source_y) * 2 + lax.rem(r + rr, 2)
                 xperm[xs_ * 16 + k * 2 + rr] = xblk[order[j]]
 
+    shares[1].wait_recv()
+    shares[2].start()
+
     pltpu.make_async_copy(hr.at[pl.ds(1, QPEERS - 1)], hr.at[pl.ds(1, QPEERS - 1)], h_recv).wait()
+    ring_advance()
     wide = hr[...].astype(F32)
     left = jnp.concatenate([wide[:, 8 * m : 8 * m + 8, :].reshape(QPEERS * TOKENS, 128) for m in range(4)], axis=1).astype(BF16)
-    for m in range(3):
-        pltpu.make_async_copy(wq.at[0, pl.ds(0, ROWS)], wq.at[0, pl.ds(0, ROWS)], wq_recv.at[m]).wait()
+    shares[0].wait_recv()
+    shares[2].wait_recv()
     partial = jnp.dot(left, wq[...].reshape(512, IN_COLUMNS), preferred_element_type=F32).reshape(QPEERS, TOKENS, IN_COLUMNS)
     packed = jnp.concatenate([partial[:, :, :384], partial[:, :, 384:]], axis=1).astype(BF16)
     pr[0] = packed[0]
     ps[...] = packed
 
-    def send_p(d, carry):
+    def send_p(i, carry):
+        d = far_first(i)
         pltpu.make_async_remote_copy(
             src_ref=ps.at[d],
             dst_ref=pr.at[d],
@@ -257,18 +280,10 @@
         ).start()
         return carry
 
-    lax.fori_loop(1, QPEERS, send_p, 0)
+    lax.fori_loop(0, QPEERS - 1, send_p, 0)
     pending.append(pltpu.make_async_copy(ps.at[pl.ds(1, QPEERS - 1)], ps.at[pl.ds(1, QPEERS - 1)], p_send).wait)
-    for k in range(1, 4):
-        up[k - 1].wait_recv()
-        up[k].start()
-        to_twin[k].start()
-        down[k - 1].wait_recv()
-        if k < 3:
-            down[k].start()
-        to_twin[8 - k].start()
-    up[3].wait_recv()
-    to_twin[4].start()
+    ring_advance()
+    ring_advance()
     pltpu.make_async_copy(pr.at[pl.ds(1, QPEERS - 1)], pr.at[pl.ds(1, QPEERS - 1)], p_recv).wait()
     projected = jnp.sum(pr[...].astype(F32), axis=0) * np.float32(1.0 / np.sqrt(np.float32(MODEL_WIDTH)))
     top, bottom = projected[0:8], projected[8:16]
@@ -279,43 +294,44 @@
     normed = raw * lax.rsqrt(jnp.mean(raw * raw, axis=1, keepdims=True) + norm_epsilon)
     cosine5 = jnp.concatenate([cosine] * 5, axis=0)
     sine5 = jnp.concatenate([sine] * 5, axis=0)
-    rotated = (normed * cosine5 + pltpu.roll(normed, HEAD_SIZE // 2, 1) * sine5).astype(BF16)
-    queries = rotated[0:32]
-    new_keys = rotated[32:40]
+    rotated = normed * cosine5 + pltpu.roll(normed, HEAD_SIZE // 2, 1) * sine5
+    qh[...] = rotated[0:32]
+    new_keys = rotated[32:40].astype(BF16)
 
     scale = HEAD_SIZE ** (-0.5)
     contract_last = (((1,), (1,)), ((), ()))
+    q_step = lax.rem(lax.broadcasted_iota(jnp.int32, (16, TOKENS), 0), STEPS)
+    k_token = lax.broadcasted_iota(jnp.int32, (16, TOKENS), 1)
+    slot = lax.broadcasted_iota(jnp.int32, (16, CACHE_SLOTS), 1)
     loads[6].wait()
     loads[7].wait()
-    q_token = lax.rem(lax.broadcasted_iota(jnp.int32, (32, TOKENS), 0), 8)
-    k_token = lax.broadcasted_iota(jnp.int32, (32, TOKENS), 1)
-    recent = lax.dot_general(queries, new_keys, contract_last, preferred_element_type=F32) * scale
-    seen = (lax.rem(q_token, 2) == lax.rem(k_token, 2)) & (lax.div(k_token, 2) <= lax.div(q_token, 2))
-    recent = jnp.where(seen, jnp.exp(recent), 0.0)
-    total = jnp.sum(recent, axis=1, keepdims=True)
-    heads = jnp.dot(recent.astype(BF16), new_values, preferred_element_type=F32)
-    slot = lax.broadcasted_iota(jnp.int32, (32, CACHE_SLOTS), 1)
-    row_of = lax.rem(lax.broadcasted_iota(jnp.int32, (32, CACHE_SLOTS), 0), 2)
     for n in range(2):
+        rows = pl.ds(n, 16, stride=2)
+        queries = qh[rows, :].astype(BF16)
+        recent = lax.dot_general(queries, new_keys, contract_last, preferred_element_type=F32) * scale
+        seen = (lax.rem(k_token, 2) == n) & (lax.div(k_token, 2) <= q_step)
+        recent = jnp.where(seen, jnp.exp(recent), 0.0)
         scores = (
             lax.dot_general(queries, keys_v[n * CACHE_SLOTS : (n + 1) * CACHE_SLOTS, :], contract_last, preferred_element_type=F32)
             * scale
         )
-        past = jnp.where((slot < lengths[n]) & (row_of == n), jnp.exp(scores), 0.0)
-        total = total + jnp.sum(past, axis=1, keepdims=True)
-        heads = heads + jnp.dot(
+        past = jnp.where(slot < lengths[n], jnp.exp(scores), 0.0)
+        total = jnp.sum(past, axis=1, keepdims=True) + jnp.sum(recent, axis=1, keepdims=True)
+        heads = jnp.dot(
             past.astype(BF16), values_v[n * CACHE_SLOTS : (n + 1) * CACHE_SLOTS, :], preferred_element_type=F32
-        )
-    heads = (heads / total).astype(BF16)
+        ) + jnp.dot(recent.astype(BF16), new_values, preferred_element_type=F32)
+        hh[rows, :] = heads / total
+    heads = hh[...].astype(BF16)
 
     os[...] = heads
     orr[0] = heads
-    for d in range(1, 4):
+    for d in (2, 1, 3):
         copy = pltpu.make_async_remote_copy(
             src_ref=os, dst_ref=orr.at[d], send_sem=o_send.at[d - 1], recv_sem=o_recv.at[d - 1], device_id=y_peer(d), device_id_type=MESH
         )
         copy.start()
         pending.append(copy.wait_send)
+    ring_advance()
     for k in range(8):
         to_twin[k].wait_recv()
     for d in range(3):
@@ -326,7 +342,7 @@
     attn = attn * np.float32(1.0 / np.sqrt(np.float32(KEY_VALUE_HEADS * OUT_COLUMNS)))
     attn = attn.reshape(4, 8, 1280)
     s4[...] = jnp.concatenate([attn[:, :, :640], attn[:, :, 640:]], axis=1).astype(BF16)
-    for e in range(1, 4):
+    for e in (2, 1, 3):
         copy = pltpu.make_async_remote_copy(
             src_ref=s4.at[lax.rem(xx + e, 4)],
             dst_ref=r4.at[e - 1],
@@ -358,7 +374,7 @@
     def own_copy():
         return pltpu.make_async_copy(s5, r5.at[t], r5_recv)
 
-    for e in range(1, 8):
+    for e in (4, 3, 5, 2, 6, 1, 7):
         to_owner(e).start()
         pending.append(to_owner(e).wait_send)
     pending.append(lambda: pl.when(xx != 0)(to_owner(0).wait_send))
@@ -397,6 +413,18 @@
         wait()
 
 
+def finish(master_in, mixed_in, master_out, mixed_out, held, sem):
+    write_master = pltpu.make_async_copy(master_in, master_out, sem.at[0])
+    write_master.start()
+    values = mixed_in[...].astype(F32)
+    for s in range(STEPS):
+        held[s] = values[2 * s : 2 * s + 2].astype(BF16)
+    write_mixed = pltpu.make_async_copy(held, mixed_out, sem.at[1])
+    write_mixed.start()
+    write_mixed.wait()
+    write_master.wait()
+
+
 def body(
     master, adam_first_moment, adam_second_moment, gradient, resync_order, inputs, in_gain, post_gain, lengths,
     cached_key_rows, cached_value_rows,
@@ -410,9 +438,9 @@
     flat = (ROWS * 10, 128)
     new_master, mixed = pl.pallas_call(
         kernel,
-        out_shape=(jax.ShapeDtypeStruct(flat, F32), jax.ShapeDtypeStruct((TOKENS, 640), BF16)),
+        out_shape=(pltpu.VMEM(flat, F32), pltpu.VMEM((TOKENS, 640), BF16)),
         in_specs=[hbm] * 12,
-        out_specs=(hbm, vmem),
+        out_specs=(vmem, vmem),
         scratch_shapes=[
             pltpu.SMEM((BLOCKS,), jnp.int32),
             pltpu.SMEM((2,), jnp.int32),
@@ -421,6 +449,8 @@
             pltpu.VMEM((STEPS, 2, MODEL_WIDTH), BF16),
             pltpu.VMEM((1, MODEL_WIDTH), F32),
             pltpu.VMEM((TOKENS, MODEL_WIDTH), F32),
+            pltpu.VMEM((32, HEAD_SIZE), F32),
+            pltpu.VMEM((32, HEAD_SIZE), F32),
             pltpu.VMEM((BLOCKS, TOKENS, 128), F32),
             pltpu.VMEM((BLOCKS, TOKENS, 128), F32),
             pltpu.VMEM((BLOCKS, TOKENS, 128), F32),
@@ -443,7 +473,7 @@
             pltpu.VMEM((3, 16, 640), BF16),
             pltpu.VMEM((16, 640), BF16),
             pltpu.VMEM((8, 16, 640), BF16),
-            dma((12,)), dma, dma, dma, dma((3,)), dma((3,)), dma((7,)), dma((7,)), dma((8,)), dma((8,)),
+            dma((12,)), dma, dma, dma((3,)), dma((3,)), dma((7,)), dma((7,)), dma((8,)), dma((8,)),
             dma, dma, dma((3,)), dma((3,)), dma((3,)), dma((3,)), dma((8,)), dma, dma,
         ],
         compiler_params=pltpu.CompilerParams(collective_id=0, has_side_effects=True, vmem_limit_bytes=56 << 20),
@@ -454,7 +484,15 @@
         master.reshape(flat), adam_first_moment.reshape(flat), adam_second_moment.reshape(flat), gradient.reshape(ROWS, 1280),
         cached_key_rows.reshape(2 * CACHE_SLOTS, HEAD_SIZE), cached_value_rows.reshape(2 * CACHE_SLOTS, HEAD_SIZE),
     )
-    return new_master.reshape(ROWS, 1, 1280), mixed.reshape(STEPS, 2, 640)
+    new_master, mixed = pl.pallas_call(
+        finish,
+        out_shape=(jax.ShapeDtypeStruct(flat, F32), jax.ShapeDtypeStruct((STEPS, 2, 640), BF16)),
+        in_specs=[vmem, vmem],
+        out_specs=(hbm, hbm),
+        scratch_shapes=[pltpu.VMEM((STEPS, 2, 640), BF16), dma((2,))],
+        name="finish",
+    )(new_master, mixed)
+    return new_master.reshape(ROWS, 1, 1280), mixed
 
 
 def solution(mesh):

time: 58.9 us -> 53.2 us (0.903)
  Pallas kernels: 54.5 us -> 50.5 us
  local copies, waits for them, and re-layouts: 3.11 us -> 1.33 us
    pallas_call x1 -> x2, Pallas kernels: 54.5 us -> 50.5 us  [the longest x1 48.7 us: body(): pl.pallas_call(kernel, out_shape=(pltpu.VMEM(flat, F32), pltpu.VMEM((TOKE...]
    reshape x1 -> x0, local copies, waits for them, and re-layouts: 1.31 us -> none  [body(): return (new_master.reshape(ROWS, 1, 1280), mixed.reshape(STEPS, 2, 640))]
    unnamed x1 -> x4, local copies, waits for them, and re-layouts: 1.8 us -> 1.33 us
where the time goes in v3:
time: 53.2 us; the launch traced here: 52.5 us
  Pallas kernels  50.5 us (95%)
  local copies, waits for them, and re-layouts  1.33 us (2%)
  between operations  0.65 us (1%)
    pallas_call x1, Pallas kernels, body(): pl.pallas_call(kernel, out_shape=(pltpu.VMEM(flat, F32), pltpu.VMEM((TOKE...  48.7 us
    pallas_call x1, Pallas kernels, body(): pl.pallas_call(finish, out_shape=(jax.ShapeDtypeStruct(flat, F32), jax.Sh...  1.77 us
    unnamed x4, local copies, waits for them, and re-layouts  1.33 us

profile of v3, /device:TPU:6, one launch (start us, length us, event | category | flops | bytes accessed | tf_op | source)
XLA Modules:
  0.0 52.5 jit_solution(4321425369692576371)
XLA Ops:
  0.6 48.7 %adam_attention.1 = (f32[800,128]{1,0:T(8,128)S(1)}, bf16[8,640]{1,0:T(8,128)(2,1)S(1)}) custom-call(s32[64]{0:T(128)} %order_in.1, s32[2]{0:T(128)} %lengths_in.1, bf16[4,2,5120]{2,1,0:T(2,128)(2,1)} %x_in.1, f32[1,5120]{1,0:T(1,128)} %bitcast.14, f32[640]{0:T(1024)} %post_in.1, f32[1,128]{1,0:T(1,128)} %constant.2.clone.freq_in, f32[800,128]{1,0:T(8,128)} %bitcast.10, ...), custom_call_target="tpu_custom_call" | custom-call | flops 400000000 | bytes 4500000 | tf_op jit(solution)/shard_map/adam_attention/pallas_call | solution.py:439
  49.3 0.0 copy-start
  49.4 0.7 %copy-done = f32[800,128]{1,0:T(8,128)} copy-done((f32[800,128]{1,0:T(8,128)}, f32[800,128]{1,0:T(8,128)S(1)}, u32[]{:S(2)}) %copy-start) | copy-done | bytes 409624
  50.1 0.0 copy-start.1
  50.1 0.6 %copy-done.1 = bf16[8,640]{1,0:T(8,128)(2,1)} copy-done((bf16[8,640]{1,0:T(8,128)(2,1)}, bf16[8,640]{1,0:T(8,128)(2,1)S(1)}, u32[]{:S(2)}) %copy-start.1) | copy-done | bytes 10264
  50.7 1.8 %finish.1 = (f32[800,128]{1,0:T(8,128)}, bf16[4,2,640]{2,1,0:T(2,128)(2,1)}) custom-call(f32[800,128]{1,0:T(8,128)} %copy-done, bf16[8,640]{1,0:T(8,128)(2,1)} %copy-done.1), custom_call_target="tpu_custom_call" | custom-call | tf_op jit(solution)/shard_map/finish/pallas_call | solution.py:487
Async XLA Ops:
  49.3 0.8 %copy-start = (f32[800,128]{1,0:T(8,128)}, f32[800,128]{1,0:T(8,128)S(1)}, u32[]{:S(2)}) copy-start(f32[800,128]{1,0:T(8,128)S(1)} %get-tuple-element.6.master_in) | copy-start | bytes 1228804
  50.1 0.6 %copy-start.1 = (bf16[8,640]{1,0:T(8,128)(2,1)}, bf16[8,640]{1,0:T(8,128)(2,1)S(1)}, u32[]{:S(2)}) copy-start(bf16[8,640]{1,0:T(8,128)(2,1)S(1)} %get-tuple-element.7.mixed_in) | copy-start | bytes 30724

commit v4 on v3

--- a/solution.py
+++ b/solution.py
@@ -94,31 +94,36 @@
             ]
         )
     ]
-    for load in loads:
-        load.start()
+    for i in (0, 1, 8):
+        loads[i].start()
 
     barrier = pltpu.get_barrier_semaphore()
 
     def greet(device):
         pl.semaphore_signal(barrier, inc=1, device_id=device, device_id_type=MESH)
 
-    def greet_q(d, carry):
-        greet(q_peer(d))
+    def far_first(i):
+        return QPEERS // 2 + jnp.where(lax.rem(i, 2) == 1, lax.div(i + 1, 2), -lax.div(i, 2))
+
+    def greet_q(i, carry):
+        greet(q_peer(far_first(i)))
         return carry
 
-    lax.fori_loop(1, QPEERS, greet_q, 0)
-    for device in (twin, partner, above, below):
-        greet(device)
-    for d in range(1, 4):
-        greet(y_peer(d))
-        greet(x_peer(d))
-    for e in range(8):
+    lax.fori_loop(0, QPEERS - 1, greet_q, 0)
+    for e in (4, 3, 5, 2, 6, 1, 7, 0):
         there = lax.rem(t + e, 8)
         device = dev(z, lax.rem(y + lax.div(there, 2), 4), r, there)
         if e == 0:
             pl.when(xx != 0)(functools.partial(greet, device))
         else:
             greet(device)
+    for d in (2, 1, 3):
+        greet(y_peer(d))
+        greet(x_peer(d))
+    for device in (partner, above, below, twin):
+        greet(device)
+    for i in (2, 3, 4, 5, 6, 7, 9, 10, 11):
+        loads[i].start()
     greetings = (QPEERS - 1) + 4 + 6 + 7 + jnp.where(xx != 0, 1, 0)
 
     loads[0].wait()
@@ -161,9 +166,6 @@
 
     pl.semaphore_wait(barrier, greetings)
 
-    def far_first(i):
-        return QPEERS // 2 + jnp.where(lax.rem(i, 2) == 1, lax.div(i + 1, 2), -lax.div(i, 2))
-
     def send_h(i, carry):
         d = far_first(i)
         pltpu.make_async_remote_copy(
@@ -257,8 +259,8 @@
     shares[1].wait_recv()
     shares[2].start()
 
+    ring_advance()
     pltpu.make_async_copy(hr.at[pl.ds(1, QPEERS - 1)], hr.at[pl.ds(1, QPEERS - 1)], h_recv).wait()
-    ring_advance()
     wide = hr[...].astype(F32)
     left = jnp.concatenate([wide[:, 8 * m : 8 * m + 8, :].reshape(QPEERS * TOKENS, 128) for m in range(4)], axis=1).astype(BF16)
     shares[0].wait_recv()
@@ -490,8 +492,9 @@
         in_specs=[vmem, vmem],
         out_specs=(hbm, hbm),
         scratch_shapes=[pltpu.VMEM((STEPS, 2, 640), BF16), dma((2,))],
+        compiler_params=pltpu.CompilerParams(vmem_limit_bytes=2 << 20),
         name="finish",
-    )(new_master, mixed)
+    )(pltpu.with_memory_space_constraint(new_master, pltpu.VMEM), pltpu.with_memory_space_constraint(mixed, pltpu.VMEM))
     return new_master.reshape(ROWS, 1, 1280), mixed
 
 

time: 53.2 us -> 50.2 us (0.944)
  Pallas kernels: 50.5 us -> 49 us
  local copies, waits for them, and re-layouts: 1.33 us -> 0 us
    unnamed x4 -> x0, local copies, waits for them, and re-layouts: 1.33 us -> none
    pallas_call x1, Pallas kernels: 1.77 us -> 0.77 us  [body(): pl.pallas_call(finish, out_shape=(jax.ShapeDtypeStruct(flat, F32), jax.Sh...]
where the time goes in v4:
time: 50.2 us; the launch traced here: 49.7 us
  Pallas kernels  49 us (98%)
  between operations  0.64 us (1%)
    pallas_call x1, Pallas kernels, body(): pl.pallas_call(kernel, out_shape=(pltpu.VMEM(flat, F32), pltpu.VMEM((TOKE...  48.3 us

profile of v4, /device:TPU:6, one launch (start us, length us, event | category | flops | bytes accessed | tf_op | source)
XLA Modules:
  0.0 49.7 jit_solution(4841238483234148813)
XLA Ops:
  0.6 48.3 %adam_attention.1 = (f32[800,128]{1,0:T(8,128)S(1)}, bf16[8,640]{1,0:T(8,128)(2,1)S(1)}) custom-call(s32[64]{0:T(128)} %order_in.1, s32[2]{0:T(128)} %lengths_in.1, bf16[4,2,5120]{2,1,0:T(2,128)(2,1)} %x_in.1, f32[1,5120]{1,0:T(1,128)} %bitcast.14, f32[640]{0:T(1024)} %post_in.1, f32[1,128]{1,0:T(1,128)} %constant.2.clone.freq_in, f32[800,128]{1,0:T(8,128)} %bitcast.10, ...), custom_call_target="tpu_custom_call" | custom-call | flops 400000000 | bytes 4500000 | tf_op jit(solution)/shard_map/adam_attention/pallas_call | solution.py:441
  48.9 0.8 %finish.1 = (f32[800,128]{1,0:T(8,128)}, bf16[4,2,640]{2,1,0:T(2,128)(2,1)}) custom-call(f32[800,128]{1,0:T(8,128)S(1)} %get-tuple-element.6.master_in, bf16[8,640]{1,0:T(8,128)(2,1)S(1)} %get-tuple-element.7.mixed_in), custom_call_target="tpu_custom_call" | custom-call | tf_op jit(solution)/shard_map/finish/pallas_call | solution.py:489

commit v5 on v4

--- a/solution.py
+++ b/solution.py
@@ -56,7 +56,7 @@
     order, lengths, post_v, freq_v, x_v, gain_v, xs, qh, hh, xblk, hblk, xperm, zblk, master_v, first_v, second_v, gradient_v, keys_v, values_v,
     hs, hr, wq, wo, ps, pr, os, orr, s4, r4, s5, r5,
     load_sem, h_send, h_recv, wq_send, wq_recv, ring_send, ring_recv, twin_send, twin_recv,
-    p_send, p_recv, o_send, o_recv, r4_send, r4_recv, r5_send, r5_self, r5_recv,
+    p_send, p_recv, o_send, o_recv, r4_send, r4_recv, r5_send, r5_recv,
 ):
     l, r, t = lax.axis_index("learn"), lax.axis_index("rep"), lax.axis_index("tp")
     z, y = lax.div(l, 4), lax.rem(l, 4)
@@ -69,15 +69,15 @@
 
     def q_peer(d):
         other = lax.rem(c + d, QPEERS)
-        return dev(lax.div(other, 2), lax.rem(other, 2) * 2 + yy, r, t)
+        return dev(lax.div(other, 2), lax.rem(other, 2) * 2 + yy, 1 - r, t)
 
     twin = dev(z, y, 1 - r, t)
-    partner = dev(z, yp * 2 + 1 - yy, r, t)
-    above = dev(lax.rem(z + 1, 8), y, r, t)
-    below = dev(lax.rem(z + 7, 8), y, r, t)
+    partner = dev(z, yp * 2 + 1 - yy, 1 - r, t)
+    above = dev(lax.rem(z + 1, 8), y, 1 - r, t)
+    below = dev(lax.rem(z + 7, 8), y, 1 - r, t)
 
     def y_peer(d):
-        return dev(z, lax.rem(y + d, 4), r, t)
+        return dev(z, lax.rem(y + d, 4), 1 - r, t)
 
     def x_peer(e):
         return dev(z, y, r, lax.rem(xx + e, 4) * 2 + yh)
@@ -103,29 +103,22 @@
         pl.semaphore_signal(barrier, inc=1, device_id=device, device_id_type=MESH)
 
     def far_first(i):
-        return QPEERS // 2 + jnp.where(lax.rem(i, 2) == 1, lax.div(i + 1, 2), -lax.div(i, 2))
+        return lax.rem(QPEERS // 2 + jnp.where(lax.rem(i, 2) == 1, lax.div(i + 1, 2), -lax.div(i, 2)), QPEERS)
 
     def greet_q(i, carry):
         greet(q_peer(far_first(i)))
         return carry
 
-    lax.fori_loop(0, QPEERS - 1, greet_q, 0)
+    lax.fori_loop(0, QPEERS, greet_q, 0)
     for e in (4, 3, 5, 2, 6, 1, 7, 0):
         there = lax.rem(t + e, 8)
-        device = dev(z, lax.rem(y + lax.div(there, 2), 4), r, there)
-        if e == 0:
-            pl.when(xx != 0)(functools.partial(greet, device))
-        else:
-            greet(device)
+        greet(dev(z, lax.rem(y + lax.div(there, 2), 4), 1 - r, there))
     for d in (2, 1, 3):
-        greet(y_peer(d))
         greet(x_peer(d))
-    for device in (partner, above, below, twin):
+    for device in (y_peer(1), y_peer(3), above, below, partner):
         greet(device)
     for i in (2, 3, 4, 5, 6, 7, 9, 10, 11):
         loads[i].start()
-    greetings = (QPEERS - 1) + 4 + 6 + 7 + jnp.where(xx != 0, 1, 0)
-
     loads[0].wait()
     loads[1].wait()
     loads[8].wait()
@@ -142,13 +135,9 @@
         parts = []
         for m in range(4):
             my, mr = m // 2, m % 2
-            w = lax.rem(yy + my, 2) * 2 + lax.rem(r + mr, 2)
+            w = lax.rem(yy + my, 2) * 2 + lax.rem(1 - r + mr, 2)
             parts.append(hblk[order[other * 4 + w]])
-        piece = jnp.concatenate(parts, axis=0).astype(BF16)
-        if d == 0:
-            hr[0] = piece
-        else:
-            hs[d] = piece
+        hs[d] = jnp.concatenate(parts, axis=0).astype(BF16)
 
     wq[:, ROWS:, :] = jnp.zeros((4, 128 - ROWS, IN_COLUMNS), BF16)
     for i in range(2, 6):
@@ -164,7 +153,7 @@
         else:
             wo[0, 0, :, (j - 6) * 128 : (j - 5) * 128] = fresh.astype(BF16)
 
-    pl.semaphore_wait(barrier, greetings)
+    pl.semaphore_wait(barrier, QPEERS + 8 + 3 + 5)
 
     def send_h(i, carry):
         d = far_first(i)
@@ -173,8 +162,8 @@
         ).start()
         return carry
 
-    lax.fori_loop(0, QPEERS - 1, send_h, 0)
-    pending.append(pltpu.make_async_copy(hs.at[pl.ds(1, QPEERS - 1)], hs.at[pl.ds(1, QPEERS - 1)], h_send).wait)
+    lax.fori_loop(0, QPEERS, send_h, 0)
+    pending.append(pltpu.make_async_copy(hs, hs, h_send).wait)
 
     def share(src, dst, device):
         return pltpu.make_async_remote_copy(
@@ -186,27 +175,27 @@
             device_id_type=MESH,
         )
 
-    shares = [share(0, 1, twin), share(0, 2, partner), share(2, 3, twin)]
+    shares = [share(0, 1, twin), share(0, 3, partner), share(3, 2, twin)]
     pending.extend(copy.wait_send for copy in shares)
     shares[1].start()
     shares[0].start()
 
-    def ring(src, dst, index, device):
+    def ring(src, dst, index, device, rows=pl.ds(0, ROWS)):
         return pltpu.make_async_remote_copy(
-            src_ref=wo.at[src, 0],
-            dst_ref=wo.at[dst, 0],
+            src_ref=wo.at[src, src % 2, rows],
+            dst_ref=wo.at[dst, dst % 2, rows],
             send_sem=ring_send.at[index],
             recv_sem=ring_recv.at[index],
             device_id=device,
             device_id_type=MESH,
         )
 
-    up = [ring(k, k + 1, k, above) for k in range(4)]
-    down = [ring((8 - k) % 8, 7 - k, 4 + k, below) for k in range(3)]
+    up = [ring(k, k + 1, k, above) for k in range(3)] + [ring(3, 4, 3, above, pl.ds(0, 48))]
+    down = [ring((8 - k) % 8, 7 - k, 4 + k, below) for k in range(3)] + [ring(5, 4, 7, below, pl.ds(48, ROWS - 48))]
     to_twin = [
         pltpu.make_async_remote_copy(
-            src_ref=wo.at[k, 0],
-            dst_ref=wo.at[k, 1],
+            src_ref=wo.at[k, k % 2],
+            dst_ref=wo.at[k, 1 - k % 2],
             send_sem=twin_send.at[k],
             recv_sem=twin_recv.at[k],
             device_id=twin,
@@ -223,9 +212,9 @@
         up[k - 1].wait_recv()
         if k < 4:
             up[k].start()
-            down[k - 1].wait_recv()
-            if k < 3:
-                down[k].start()
+        down[k - 1].wait_recv()
+        if k < 4:
+            down[k].start()
             to_twin[8 - k].start()
         to_twin[k].start()
 
@@ -253,21 +242,20 @@
         source_y = lax.rem(y + xs_, 4)
         for k in range(8):
             for rr in range(2):
-                j = (lax.rem(z + 8 - k, 8) * 4 + source_y) * 2 + lax.rem(r + rr, 2)
+                j = (lax.rem(z + 8 - k, 8) * 4 + source_y) * 2 + lax.rem(1 - r + rr, 2)
                 xperm[xs_ * 16 + k * 2 + rr] = xblk[order[j]]
 
     shares[1].wait_recv()
     shares[2].start()
 
     ring_advance()
-    pltpu.make_async_copy(hr.at[pl.ds(1, QPEERS - 1)], hr.at[pl.ds(1, QPEERS - 1)], h_recv).wait()
+    pltpu.make_async_copy(hr, hr, h_recv).wait()
     wide = hr[...].astype(F32)
     left = jnp.concatenate([wide[:, 8 * m : 8 * m + 8, :].reshape(QPEERS * TOKENS, 128) for m in range(4)], axis=1).astype(BF16)
     shares[0].wait_recv()
     shares[2].wait_recv()
     partial = jnp.dot(left, wq[...].reshape(512, IN_COLUMNS), preferred_element_type=F32).reshape(QPEERS, TOKENS, IN_COLUMNS)
     packed = jnp.concatenate([partial[:, :, :384], partial[:, :, 384:]], axis=1).astype(BF16)
-    pr[0] = packed[0]
     ps[...] = packed
 
     def send_p(i, carry):
@@ -282,11 +270,11 @@
         ).start()
         return carry
 
-    lax.fori_loop(0, QPEERS - 1, send_p, 0)
-    pending.append(pltpu.make_async_copy(ps.at[pl.ds(1, QPEERS - 1)], ps.at[pl.ds(1, QPEERS - 1)], p_send).wait)
+    lax.fori_loop(0, QPEERS, send_p, 0)
+    pending.append(pltpu.make_async_copy(ps, ps, p_send).wait)
     ring_advance()
     ring_advance()
-    pltpu.make_async_copy(pr.at[pl.ds(1, QPEERS - 1)], pr.at[pl.ds(1, QPEERS - 1)], p_recv).wait()
+    pltpu.make_async_copy(pr, pr, p_recv).wait()
     projected = jnp.sum(pr[...].astype(F32), axis=0) * np.float32(1.0 / np.sqrt(np.float32(MODEL_WIDTH)))
     top, bottom = projected[0:8], projected[8:16]
     raw = jnp.concatenate(
@@ -326,17 +314,16 @@
     heads = hh[...].astype(BF16)
 
     os[...] = heads
-    orr[0] = heads
-    for d in (2, 1, 3):
+    for d in (2, 1, 3, 0):
         copy = pltpu.make_async_remote_copy(
-            src_ref=os, dst_ref=orr.at[d], send_sem=o_send.at[d - 1], recv_sem=o_recv.at[d - 1], device_id=y_peer(d), device_id_type=MESH
+            src_ref=os, dst_ref=orr.at[d], send_sem=o_send.at[d], recv_sem=o_recv.at[d], device_id=y_peer(d), device_id_type=MESH
         )
         copy.start()
         pending.append(copy.wait_send)
     ring_advance()
     for k in range(8):
         to_twin[k].wait_recv()
-    for d in range(3):
+    for d in range(4):
         pltpu.make_async_copy(os, os, o_recv.at[d]).wait()
     wide = orr[...].astype(F32)
     left = jnp.concatenate([wide[:, 8 * h : 8 * h + 8, :].reshape(32, 128) for h in range(4)], axis=1).astype(BF16)
@@ -369,26 +356,13 @@
             dst_ref=r5.at[t],
             send_sem=r5_send.at[e],
             recv_sem=r5_recv,
-            device_id=dev(z, target_y, r, there),
-            device_id_type=MESH,
-        )
-
-    def own_copy():
-        return pltpu.make_async_copy(s5, r5.at[t], r5_recv)
-
-    for e in (4, 3, 5, 2, 6, 1, 7):
+            device_id=dev(z, target_y, 1 - r, there),
+            device_id_type=MESH,
+        )
+
+    for e in (4, 3, 5, 2, 6, 1, 7, 0):
         to_owner(e).start()
         pending.append(to_owner(e).wait_send)
-    pending.append(lambda: pl.when(xx != 0)(to_owner(0).wait_send))
-
-    @pl.when(xx != 0)
-    def _():
-        to_owner(0).start()
-
-    @pl.when(xx == 0)
-    def _():
-        own_copy().start()
-
     pltpu.make_async_copy(r5, r5, r5_recv).wait()
 
     squares = jnp.zeros((TOKENS, 128), F32)
@@ -407,7 +381,7 @@
         j = stored[i]
         k = lax.rem(z + 8 - lax.div(j, 8), 8)
         source = lax.rem(lax.rem(lax.div(j, 2), 4) + 4 - y, 4)
-        rr = lax.rem(lax.rem(j, 2) + r, 2)
+        rr = lax.rem(lax.rem(j, 2) + 1 - r, 2)
         pieces.append(zblk[source * 16 + k * 2 + rr][:, :ROWS])
     mixed_out[...] = (jnp.concatenate(pieces, axis=1) * rscale * post_v[...].reshape(1, 640)).astype(BF16)
 
@@ -475,8 +449,8 @@
             pltpu.VMEM((3, 16, 640), BF16),
             pltpu.VMEM((16, 640), BF16),
             pltpu.VMEM((8, 16, 640), BF16),
-            dma((12,)), dma, dma, dma((3,)), dma((3,)), dma((7,)), dma((7,)), dma((8,)), dma((8,)),
-            dma, dma, dma((3,)), dma((3,)), dma((3,)), dma((3,)), dma((8,)), dma, dma,
+            dma((12,)), dma, dma, dma((3,)), dma((3,)), dma((8,)), dma((8,)), dma((8,)), dma((8,)),
+            dma, dma, dma((4,)), dma((4,)), dma((3,)), dma((3,)), dma((8,)), dma,
         ],
         compiler_params=pltpu.CompilerParams(collective_id=0, has_side_effects=True, vmem_limit_bytes=56 << 20),
         cost_estimate=pl.CostEstimate(flops=400_000_000, bytes_accessed=4_500_000, transcendentals=200_000),

time: 50.2 us -> 52.2 us (1.040)
  the two profiles are of different devices: /device:TPU:6 before, /device:TPU:1 now
where the time goes in v5:
time: 52.2 us; the launch traced here: 52 us
  Pallas kernels  51.4 us (98%)
  between operations  0.64 us (1%)
    pallas_call x1, Pallas kernels, body(): pl.pallas_call(kernel, out_shape=(pltpu.VMEM(flat, F32), pltpu.VMEM((TOKE...  50.6 us

profile of v5, /device:TPU:1, one launch (start us, length us, event | category | flops | bytes accessed | tf_op | source)
XLA Modules:
  0.0 52.0 jit_solution(8500535565717382526)
XLA Ops:
  0.6 50.6 %adam_attention.1 = (f32[800,128]{1,0:T(8,128)S(1)}, bf16[8,640]{1,0:T(8,128)(2,1)S(1)}) custom-call(s32[64]{0:T(128)} %order_in.1, s32[2]{0:T(128)} %lengths_in.1, bf16[4,2,5120]{2,1,0:T(2,128)(2,1)} %x_in.1, f32[1,5120]{1,0:T(1,128)} %bitcast.14, f32[640]{0:T(1024)} %post_in.1, f32[1,128]{1,0:T(1,128)} %constant.2.clone.freq_in, f32[800,128]{1,0:T(8,128)} %bitcast.10, ...), custom_call_target="tpu_custom_call" | custom-call | flops 400000000 | bytes 4500000 | tf_op jit(solution)/shard_map/adam_attention/pallas_call | solution.py:415
  51.2 0.8 %finish.1 = (f32[800,128]{1,0:T(8,128)}, bf16[4,2,640]{2,1,0:T(2,128)(2,1)}) custom-call(f32[800,128]{1,0:T(8,128)S(1)} %get-tuple-element.6.master_in, bf16[8,640]{1,0:T(8,128)(2,1)S(1)} %get-tuple-element.7.mixed_in), custom_call_target="tpu_custom_call" | custom-call | tf_op jit(solution)/shard_map/finish/pallas_call | solution.py:463

commit v6 on v5

--- a/solution.py
+++ b/solution.py
@@ -77,7 +77,7 @@
     below = dev(lax.rem(z + 7, 8), y, 1 - r, t)
 
     def y_peer(d):
-        return dev(z, lax.rem(y + d, 4), 1 - r, t)
+        return dev(z, lax.rem(y + d, 4), r, t)
 
     def x_peer(e):
         return dev(z, y, r, lax.rem(xx + e, 4) * 2 + yh)
@@ -112,10 +112,15 @@
     lax.fori_loop(0, QPEERS, greet_q, 0)
     for e in (4, 3, 5, 2, 6, 1, 7, 0):
         there = lax.rem(t + e, 8)
-        greet(dev(z, lax.rem(y + lax.div(there, 2), 4), 1 - r, there))
+        device = dev(z, lax.rem(y + lax.div(there, 2), 4), r, there)
+        if e == 0:
+            pl.when(xx != 0)(functools.partial(greet, device))
+        else:
+            greet(device)
     for d in (2, 1, 3):
+        greet(y_peer(d))
         greet(x_peer(d))
-    for device in (y_peer(1), y_peer(3), above, below, partner):
+    for device in (above, below, partner):
         greet(device)
     for i in (2, 3, 4, 5, 6, 7, 9, 10, 11):
         loads[i].start()
@@ -153,7 +158,7 @@
         else:
             wo[0, 0, :, (j - 6) * 128 : (j - 5) * 128] = fresh.astype(BF16)
 
-    pl.semaphore_wait(barrier, QPEERS + 8 + 3 + 5)
+    pl.semaphore_wait(barrier, QPEERS + 7 + 6 + 3 + jnp.where(xx != 0, 1, 0))
 
     def send_h(i, carry):
         d = far_first(i)
@@ -242,7 +247,7 @@
         source_y = lax.rem(y + xs_, 4)
         for k in range(8):
             for rr in range(2):
-                j = (lax.rem(z + 8 - k, 8) * 4 + source_y) * 2 + lax.rem(1 - r + rr, 2)
+                j = (lax.rem(z + 8 - k, 8) * 4 + source_y) * 2 + lax.rem(r + rr, 2)
                 xperm[xs_ * 16 + k * 2 + rr] = xblk[order[j]]
 
     shares[1].wait_recv()
@@ -314,16 +319,17 @@
     heads = hh[...].astype(BF16)
 
     os[...] = heads
-    for d in (2, 1, 3, 0):
+    orr[0] = heads
+    for d in (2, 1, 3):
         copy = pltpu.make_async_remote_copy(
-            src_ref=os, dst_ref=orr.at[d], send_sem=o_send.at[d], recv_sem=o_recv.at[d], device_id=y_peer(d), device_id_type=MESH
+            src_ref=os, dst_ref=orr.at[d], send_sem=o_send.at[d - 1], recv_sem=o_recv.at[d - 1], device_id=y_peer(d), device_id_type=MESH
         )
         copy.start()
         pending.append(copy.wait_send)
     ring_advance()
     for k in range(8):
         to_twin[k].wait_recv()
-    for d in range(4):
+    for d in range(3):
         pltpu.make_async_copy(os, os, o_recv.at[d]).wait()
     wide = orr[...].astype(F32)
     left = jnp.concatenate([wide[:, 8 * h : 8 * h + 8, :].reshape(32, 128) for h in range(4)], axis=1).astype(BF16)
@@ -356,13 +362,23 @@
             dst_ref=r5.at[t],
             send_sem=r5_send.at[e],
             recv_sem=r5_recv,
-            device_id=dev(z, target_y, 1 - r, there),
+            device_id=dev(z, target_y, r, there),
             device_id_type=MESH,
         )
 
-    for e in (4, 3, 5, 2, 6, 1, 7, 0):
+    for e in (4, 3, 5, 2, 6, 1, 7):
         to_owner(e).start()
         pending.append(to_owner(e).wait_send)
+    pending.append(lambda: pl.when(xx != 0)(to_owner(0).wait_send))
+
+    @pl.when(xx != 0)
+    def _():
+        to_owner(0).start()
+
+    @pl.when(xx == 0)
+    def _():
+        pltpu.make_async_copy(s5, r5.at[t], r5_recv).start()
+
     pltpu.make_async_copy(r5, r5, r5_recv).wait()
 
     squares = jnp.zeros((TOKENS, 128), F32)
@@ -381,7 +397,7 @@
         j = stored[i]
         k = lax.rem(z + 8 - lax.div(j, 8), 8)
         source = lax.rem(lax.rem(lax.div(j, 2), 4) + 4 - y, 4)
-        rr = lax.rem(lax.rem(j, 2) + 1 - r, 2)
+        rr = lax.rem(lax.rem(j, 2) + r, 2)
         pieces.append(zblk[source * 16 + k * 2 + rr][:, :ROWS])
     mixed_out[...] = (jnp.concatenate(pieces, axis=1) * rscale * post_v[...].reshape(1, 640)).astype(BF16)
 
@@ -450,7 +466,7 @@
             pltpu.VMEM((16, 640), BF16),
             pltpu.VMEM((8, 16, 640), BF16),
             dma((12,)), dma, dma, dma((3,)), dma((3,)), dma((8,)), dma((8,)), dma((8,)), dma((8,)),
-            dma, dma, dma((4,)), dma((4,)), dma((3,)), dma((3,)), dma((8,)), dma,
+            dma, dma, dma((3,)), dma((3,)), dma((3,)), dma((3,)), dma((8,)), dma,
         ],
         compiler_params=pltpu.CompilerParams(collective_id=0, has_side_effects=True, vmem_limit_bytes=56 << 20),
         cost_estimate=pl.CostEstimate(flops=400_000_000, bytes_accessed=4_500_000, transcendentals=200_000),

time: 52.2 us -> 49.4 us (0.946)
  the two profiles are of different devices: /device:TPU:1 before, /device:TPU:8 now
where the time goes in v6:
time: 49.4 us; the launch traced here: 49.2 us
  Pallas kernels  48.6 us (98%)
  between operations  0.64 us (1%)
    pallas_call x1, Pallas kernels, body(): pl.pallas_call(kernel, out_shape=(pltpu.VMEM(flat, F32), pltpu.VMEM((TOKE...  47.8 us

profile of v6, /device:TPU:8, one launch (start us, length us, event | category | flops | bytes accessed | tf_op | source)
XLA Modules:
  0.0 49.2 jit_solution(12026528867356272)
XLA Ops:
  0.6 47.8 %adam_attention.1 = (f32[800,128]{1,0:T(8,128)S(1)}, bf16[8,640]{1,0:T(8,128)(2,1)S(1)}) custom-call(s32[64]{0:T(128)} %order_in.1, s32[2]{0:T(128)} %lengths_in.1, bf16[4,2,5120]{2,1,0:T(2,128)(2,1)} %x_in.1, f32[1,5120]{1,0:T(1,128)} %bitcast.14, f32[640]{0:T(1024)} %post_in.1, f32[1,128]{1,0:T(1,128)} %constant.2.clone.freq_in, f32[800,128]{1,0:T(8,128)} %bitcast.10, ...), custom_call_target="tpu_custom_call" | custom-call | flops 400000000 | bytes 4500000 | tf_op jit(solution)/shard_map/adam_attention/pallas_call | solution.py:431
  48.5 0.8 %finish.1 = (f32[800,128]{1,0:T(8,128)}, bf16[4,2,640]{2,1,0:T(2,128)(2,1)}) custom-call(f32[800,128]{1,0:T(8,128)S(1)} %get-tuple-element.6.master_in, bf16[8,640]{1,0:T(8,128)(2,1)S(1)} %get-tuple-element.7.mixed_in), custom_call_target="tpu_custom_call" | custom-call | tf_op jit(solution)/shard_map/finish/pallas_call | solution.py:479

commit v7 on v6

--- a/solution.py
+++ b/solution.py
@@ -19,6 +19,8 @@
 IN_COLUMNS = 768
 OUT_COLUMNS = 512
 TOKENS = 8
+RING = (0, 1, 7, 2, 6, 3, 5, 4)
+PLACE = tuple(RING.index(k) for k in range(8))
 QPEERS = 16
 
 beta_one = 0.9
@@ -54,9 +56,9 @@
     order_in, lengths_in, x_in, gain_in, post_in, freq_in, master_in, first_in, second_in, gradient_in, keys_in, values_in,
     master_out, mixed_out,
     order, lengths, post_v, freq_v, x_v, gain_v, xs, qh, hh, xblk, hblk, xperm, zblk, master_v, first_v, second_v, gradient_v, keys_v, values_v,
-    hs, hr, wq, wo, ps, pr, os, orr, s4, r4, s5, r5,
+    hs, hr, wq, wo, ps, pr, ps2, pr2, os, orr, attn, s4, r4, s5, r5,
     load_sem, h_send, h_recv, wq_send, wq_recv, ring_send, ring_recv, twin_send, twin_recv,
-    p_send, p_recv, o_send, o_recv, r4_send, r4_recv, r5_send, r5_recv,
+    p_send, p_recv, p2_send, p2_recv, o_send, o_recv, r4_send, r4_recv, r5_send, r5_recv,
 ):
     l, r, t = lax.axis_index("learn"), lax.axis_index("rep"), lax.axis_index("tp")
     z, y = lax.div(l, 4), lax.rem(l, 4)
@@ -185,22 +187,24 @@
     shares[1].start()
     shares[0].start()
 
-    def ring(src, dst, index, device, rows=pl.ds(0, ROWS)):
+    parts = (pl.ds(0, 48), pl.ds(48, ROWS - 48))
+
+    def ring(src, dst, index, device, part):
         return pltpu.make_async_remote_copy(
-            src_ref=wo.at[src, src % 2, rows],
-            dst_ref=wo.at[dst, dst % 2, rows],
-            send_sem=ring_send.at[index],
-            recv_sem=ring_recv.at[index],
+            src_ref=wo.at[PLACE[src], src % 2, parts[part]],
+            dst_ref=wo.at[PLACE[dst], dst % 2, parts[part]],
+            send_sem=ring_send.at[2 * index + part],
+            recv_sem=ring_recv.at[2 * index + part],
             device_id=device,
             device_id_type=MESH,
         )
 
-    up = [ring(k, k + 1, k, above) for k in range(3)] + [ring(3, 4, 3, above, pl.ds(0, 48))]
-    down = [ring((8 - k) % 8, 7 - k, 4 + k, below) for k in range(3)] + [ring(5, 4, 7, below, pl.ds(48, ROWS - 48))]
+    up = {(k, part): ring(k, k + 1, k, above, part) for k in range(4) for part in range(2) if (k, part) != (3, 1)}
+    down = {(k, part): ring((8 - k) % 8, 7 - k, 4 + k, below, part) for k in range(4) for part in range(2) if (k, part) != (3, 0)}
     to_twin = [
         pltpu.make_async_remote_copy(
-            src_ref=wo.at[k, k % 2],
-            dst_ref=wo.at[k, 1 - k % 2],
+            src_ref=wo.at[PLACE[k], k % 2],
+            dst_ref=wo.at[PLACE[k], 1 - k % 2],
             send_sem=twin_send.at[k],
             recv_sem=twin_recv.at[k],
             device_id=twin,
@@ -208,23 +212,25 @@
         )
         for k in range(8)
     ]
-    pending.extend(copy.wait_send for copy in up + down + to_twin)
+    pending.extend(copy.wait_send for copy in list(up.values()) + list(down.values()) + to_twin)
     ring_step = [0]
 
     def ring_advance():
         ring_step[0] += 1
         k = ring_step[0]
-        up[k - 1].wait_recv()
+        for part in range(2):
+            for copies in (up, down):
+                if (k - 1, part) in copies:
+                    copies[k - 1, part].wait_recv()
+                if (k, part) in copies:
+                    copies[k, part].start()
+        to_twin[k].start()
         if k < 4:
-            up[k].start()
-        down[k - 1].wait_recv()
-        if k < 4:
-            down[k].start()
             to_twin[8 - k].start()
-        to_twin[k].start()
-
-    up[0].start()
-    down[0].start()
+
+    for part in range(2):
+        up[0, part].start()
+        down[0, part].start()
     to_twin[0].start()
 
     loads[9].wait()
@@ -243,12 +249,21 @@
         return tuple(jnp.where(actor == i, j, carry[i]) for i in range(8))
 
     stored = lax.fori_loop(0, BLOCKS, find, tuple(jnp.int32(0) for _ in range(8)))
+    places = []
+    for j in stored:
+        k = lax.rem(z + 8 - lax.div(j, 8), 8)
+        source = lax.rem(lax.rem(lax.div(j, 2), 4) + 4 - y, 4)
+        rr = lax.rem(lax.rem(j, 2) + r, 2)
+        slot = jnp.int32(0)
+        for i in range(1, 8):
+            slot = jnp.where(k == RING[i], i, slot)
+        places.append(source * 16 + slot * 2 + rr)
     for xs_ in range(4):
         source_y = lax.rem(y + xs_, 4)
         for k in range(8):
             for rr in range(2):
                 j = (lax.rem(z + 8 - k, 8) * 4 + source_y) * 2 + lax.rem(r + rr, 2)
-                xperm[xs_ * 16 + k * 2 + rr] = xblk[order[j]]
+                xperm[xs_ * 16 + PLACE[k] * 2 + rr] = xblk[order[j]]
 
     shares[1].wait_recv()
     shares[2].start()
@@ -260,38 +275,38 @@
     shares[0].wait_recv()
     shares[2].wait_recv()
     partial = jnp.dot(left, wq[...].reshape(512, IN_COLUMNS), preferred_element_type=F32).reshape(QPEERS, TOKENS, IN_COLUMNS)
-    packed = jnp.concatenate([partial[:, :, :384], partial[:, :, 384:]], axis=1).astype(BF16)
-    ps[...] = packed
-
-    def send_p(i, carry):
-        d = far_first(i)
-        pltpu.make_async_remote_copy(
-            src_ref=ps.at[d],
-            dst_ref=pr.at[d],
-            send_sem=p_send,
-            recv_sem=p_recv,
-            device_id=q_peer(QPEERS - d),
-            device_id_type=MESH,
-        ).start()
-        return carry
-
-    lax.fori_loop(0, QPEERS, send_p, 0)
-    pending.append(pltpu.make_async_copy(ps, ps, p_send).wait)
+    ps[...] = jnp.concatenate([partial[:, :, :256], partial[:, :, 256:512]], axis=1).astype(BF16)
+    ps2[...] = jnp.concatenate([partial[:, :, 512:640], partial[:, :, 640:]], axis=1).astype(BF16)
+
+    for source, target, left_sem, got_sem in ((ps, pr, p_send, p_recv), (ps2, pr2, p2_send, p2_recv)):
+
+        def send_p(i, carry):
+            d = far_first(i)
+            pltpu.make_async_remote_copy(
+                src_ref=source.at[d],
+                dst_ref=target.at[d],
+                send_sem=left_sem,
+                recv_sem=got_sem,
+                device_id=q_peer(QPEERS - d),
+                device_id_type=MESH,
+            ).start()
+            return carry
+
+        lax.fori_loop(0, QPEERS, send_p, 0)
+        pending.append(pltpu.make_async_copy(source, source, left_sem).wait)
     ring_advance()
     ring_advance()
     pltpu.make_async_copy(pr, pr, p_recv).wait()
-    projected = jnp.sum(pr[...].astype(F32), axis=0) * np.float32(1.0 / np.sqrt(np.float32(MODEL_WIDTH)))
-    top, bottom = projected[0:8], projected[8:16]
-    raw = jnp.concatenate(
-        [top[:, 0:128], top[:, 128:256], top[:, 256:384], bottom[:, 0:128], bottom[:, 128:256]], axis=0
-    )
-    new_values = bottom[:, 256:384].astype(BF16)
-    normed = raw * lax.rsqrt(jnp.mean(raw * raw, axis=1, keepdims=True) + norm_epsilon)
-    cosine5 = jnp.concatenate([cosine] * 5, axis=0)
-    sine5 = jnp.concatenate([sine] * 5, axis=0)
-    rotated = normed * cosine5 + pltpu.roll(normed, HEAD_SIZE // 2, 1) * sine5
-    qh[...] = rotated[0:32]
-    new_keys = rotated[32:40].astype(BF16)
+    in_scale = np.float32(1.0 / np.sqrt(np.float32(MODEL_WIDTH)))
+
+    def rotate(raw, count):
+        normed = raw * lax.rsqrt(jnp.mean(raw * raw, axis=1, keepdims=True) + norm_epsilon)
+        cosines = jnp.concatenate([cosine] * count, axis=0)
+        sines = jnp.concatenate([sine] * count, axis=0)
+        return normed * cosines + pltpu.roll(normed, HEAD_SIZE // 2, 1) * sines
+
+    both = jnp.sum(pr[...].astype(F32), axis=0) * in_scale
+    qh[...] = rotate(jnp.concatenate([both[0:8, 0:128], both[0:8, 128:], both[8:16, 0:128], both[8:16, 128:]], axis=0), QUERY_PER_GROUP)
 
     scale = HEAD_SIZE ** (-0.5)
     contract_last = (((1,), (1,)), ((), ()))
@@ -300,22 +315,30 @@
     slot = lax.broadcasted_iota(jnp.int32, (16, CACHE_SLOTS), 1)
     loads[6].wait()
     loads[7].wait()
+    held = []
     for n in range(2):
-        rows = pl.ds(n, 16, stride=2)
-        queries = qh[rows, :].astype(BF16)
+        queries = qh[pl.ds(n, 16, stride=2), :].astype(BF16)
+        scores = (
+            lax.dot_general(queries, keys_v[n * CACHE_SLOTS : (n + 1) * CACHE_SLOTS, :], contract_last, preferred_element_type=F32)
+            * scale
+        )
+        past = jnp.where(slot < lengths[n], jnp.exp(scores), 0.0)
+        heads = jnp.dot(
+            past.astype(BF16), values_v[n * CACHE_SLOTS : (n + 1) * CACHE_SLOTS, :], preferred_element_type=F32
+        )
+        held.append((queries, jnp.sum(past, axis=1, keepdims=True), heads))
+    pltpu.make_async_copy(pr2, pr2, p2_recv).wait()
+    both = jnp.sum(pr2[...].astype(F32), axis=0) * in_scale
+    new_keys = rotate(both[0:8], 1).astype(BF16)
+    new_values = both[8:16].astype(BF16)
+    for n in range(2):
+        queries, total, heads = held[n]
         recent = lax.dot_general(queries, new_keys, contract_last, preferred_element_type=F32) * scale
         seen = (lax.rem(k_token, 2) == n) & (lax.div(k_token, 2) <= q_step)
         recent = jnp.where(seen, jnp.exp(recent), 0.0)
-        scores = (
-            lax.dot_general(queries, keys_v[n * CACHE_SLOTS : (n + 1) * CACHE_SLOTS, :], contract_last, preferred_element_type=F32)
-            * scale
-        )
-        past = jnp.where(slot < lengths[n], jnp.exp(scores), 0.0)
-        total = jnp.sum(past, axis=1, keepdims=True) + jnp.sum(recent, axis=1, keepdims=True)
-        heads = jnp.dot(
-            past.astype(BF16), values_v[n * CACHE_SLOTS : (n + 1) * CACHE_SLOTS, :], preferred_element_type=F32
-        ) + jnp.dot(recent.astype(BF16), new_values, preferred_element_type=F32)
-        hh[rows, :] = heads / total
+        total = total + jnp.sum(recent, axis=1, keepdims=True)
+        heads = heads + jnp.dot(recent.astype(BF16), new_values, preferred_element_type=F32)
+        hh[pl.ds(n, 16, stride=2), :] = heads / total
     heads = hh[...].astype(BF16)
 
     os[...] = heads
@@ -327,16 +350,23 @@
         copy.start()
         pending.append(copy.wait_send)
     ring_advance()
-    for k in range(8):
-        to_twin[k].wait_recv()
     for d in range(3):
         pltpu.make_async_copy(os, os, o_recv.at[d]).wait()
     wide = orr[...].astype(F32)
     left = jnp.concatenate([wide[:, 8 * h : 8 * h + 8, :].reshape(32, 128) for h in range(4)], axis=1).astype(BF16)
-    attn = lax.dot_general(left, wo[...].reshape(16 * ROWS, OUT_COLUMNS), contract_last, preferred_element_type=F32)
-    attn = attn * np.float32(1.0 / np.sqrt(np.float32(KEY_VALUE_HEADS * OUT_COLUMNS)))
-    attn = attn.reshape(4, 8, 1280)
-    s4[...] = jnp.concatenate([attn[:, :, :640], attn[:, :, 640:]], axis=1).astype(BF16)
+    out_scale = np.float32(1.0 / np.sqrt(np.float32(KEY_VALUE_HEADS * OUT_COLUMNS)))
+
+    def project(half):
+        weights = wo[4 * half : 4 * half + 4].reshape(8 * ROWS, OUT_COLUMNS)
+        product = lax.dot_general(left, weights, contract_last, preferred_element_type=F32) * out_scale
+        return product.reshape(4, 8, 640)
+
+    for k in RING[:4]:
+        to_twin[k].wait_recv()
+    attn[...] = project(0)
+    for k in RING[4:]:
+        to_twin[k].wait_recv()
+    s4[...] = jnp.concatenate([attn[...], project(1)], axis=1).astype(BF16)
     for e in (2, 1, 3):
         copy = pltpu.make_async_remote_copy(
             src_ref=s4.at[lax.rem(xx + e, 4)],
@@ -355,34 +385,34 @@
     s5[...] = summed.astype(BF16)
     target_y = lax.rem(y + 4 - xx, 4)
 
-    def to_owner(e):
-        there = lax.rem(t + e, 8)
+    def to_owner(dx, flip):
         return pltpu.make_async_remote_copy(
             src_ref=s5,
             dst_ref=r5.at[t],
-            send_sem=r5_send.at[e],
-            recv_sem=r5_recv,
-            device_id=dev(z, target_y, r, there),
+            send_sem=r5_send.at[2 * dx + flip],
+            recv_sem=r5_recv.at[t],
+            device_id=dev(z, target_y, r, lax.rem(xx + dx, 4) * 2 + lax.rem(yh + flip, 2)),
             device_id_type=MESH,
         )
 
-    for e in (4, 3, 5, 2, 6, 1, 7):
-        to_owner(e).start()
-        pending.append(to_owner(e).wait_send)
-    pending.append(lambda: pl.when(xx != 0)(to_owner(0).wait_send))
+    for dx, flip in ((2, 1), (2, 0), (1, 1), (3, 1), (1, 0), (3, 0), (0, 1)):
+        to_owner(dx, flip).start()
+        pending.append(to_owner(dx, flip).wait_send)
+    pending.append(lambda: pl.when(xx != 0)(to_owner(0, 0).wait_send))
 
     @pl.when(xx != 0)
     def _():
-        to_owner(0).start()
+        to_owner(0, 0).start()
 
     @pl.when(xx == 0)
     def _():
-        pltpu.make_async_copy(s5, r5.at[t], r5_recv).start()
-
-    pltpu.make_async_copy(r5, r5, r5_recv).wait()
+        pltpu.make_async_copy(s5, r5.at[t], r5_recv.at[t]).start()
+
 
     squares = jnp.zeros((TOKENS, 128), F32)
     for xs_ in range(4):
+        for i in (2 * xs_, 2 * xs_ + 1):
+            pltpu.make_async_copy(s5, r5.at[i], r5_recv.at[i]).wait()
         both = r5[2 * xs_].astype(F32) + r5[2 * xs_ + 1].astype(F32)
         for b in range(8):
             block = widen(both[:, b * ROWS : (b + 1) * ROWS])
@@ -392,13 +422,7 @@
                 zblk[place] = residual
                 squares = squares + residual * residual
     rscale = lax.rsqrt(jnp.sum(squares, axis=1, keepdims=True) * np.float32(1.0 / MODEL_WIDTH) + norm_epsilon)
-    pieces = []
-    for i in range(8):
-        j = stored[i]
-        k = lax.rem(z + 8 - lax.div(j, 8), 8)
-        source = lax.rem(lax.rem(lax.div(j, 2), 4) + 4 - y, 4)
-        rr = lax.rem(lax.rem(j, 2) + r, 2)
-        pieces.append(zblk[source * 16 + k * 2 + rr][:, :ROWS])
+    pieces = [zblk[place][:, :ROWS] for place in places]
     mixed_out[...] = (jnp.concatenate(pieces, axis=1) * rscale * post_v[...].reshape(1, 640)).astype(BF16)
 
     for wait in pending:
@@ -457,16 +481,19 @@
             pltpu.VMEM((QPEERS, 32, 128), BF16),
             pltpu.VMEM((4, 128, IN_COLUMNS), BF16),
             pltpu.VMEM((8, 2, ROWS, OUT_COLUMNS), BF16),
-            pltpu.VMEM((QPEERS, 16, 384), BF16),
-            pltpu.VMEM((QPEERS, 16, 384), BF16),
+            pltpu.VMEM((QPEERS, 16, 256), BF16),
+            pltpu.VMEM((QPEERS, 16, 256), BF16),
+            pltpu.VMEM((QPEERS, 16, 128), BF16),
+            pltpu.VMEM((QPEERS, 16, 128), BF16),
             pltpu.VMEM((32, 128), BF16),
             pltpu.VMEM((4, 32, 128), BF16),
+            pltpu.VMEM((4, 8, 640), F32),
             pltpu.VMEM((4, 16, 640), BF16),
             pltpu.VMEM((3, 16, 640), BF16),
             pltpu.VMEM((16, 640), BF16),
             pltpu.VMEM((8, 16, 640), BF16),
-            dma((12,)), dma, dma, dma((3,)), dma((3,)), dma((8,)), dma((8,)), dma((8,)), dma((8,)),
-            dma, dma, dma((3,)), dma((3,)), dma((3,)), dma((3,)), dma((8,)), dma,
+            dma((12,)), dma, dma, dma((3,)), dma((3,)), dma((16,)), dma((16,)), dma((8,)), dma((8,)),
+            dma, dma, dma, dma, dma((3,)), dma((3,)), dma((3,)), dma((3,)), dma((8,)), dma((8,)),
         ],
         compiler_params=pltpu.CompilerParams(collective_id=0, has_side_effects=True, vmem_limit_bytes=56 << 20),
         cost_estimate=pl.CostEstimate(flops=400_000_000, bytes_accessed=4_500_000, transcendentals=200_000),

time: 49.4 us -> 49.8 us (level)
  the two profiles are of different devices: /device:TPU:8 before, /device:TPU:6 now
where the time goes in v7:
time: 49.8 us; the launch traced here: 48.8 us
  Pallas kernels  48.2 us (97%)
  between operations  0.64 us (1%)
    pallas_call x1, Pallas kernels, body(): pl.pallas_call(kernel, out_shape=(pltpu.VMEM(flat, F32), pltpu.VMEM((TOKE...  47.4 us

profile of v7, /device:TPU:6, one launch (start us, length us, event | category | flops | bytes accessed | tf_op | source)
XLA Modules:
  0.0 48.8 jit_solution(11718629028330606822)
XLA Ops:
  0.6 47.4 %adam_attention.1 = (f32[800,128]{1,0:T(8,128)S(1)}, bf16[8,640]{1,0:T(8,128)(2,1)S(1)}) custom-call(s32[64]{0:T(128)} %order_in.1, s32[2]{0:T(128)} %lengths_in.1, bf16[4,2,5120]{2,1,0:T(2,128)(2,1)} %x_in.1, f32[1,5120]{1,0:T(1,128)} %bitcast.14, f32[640]{0:T(1024)} %post_in.1, f32[1,128]{1,0:T(1,128)} %constant.2.clone.freq_in, f32[800,128]{1,0:T(8,128)} %bitcast.10, ...), custom_call_target="tpu_custom_call" | custom-call | flops 400000000 | bytes 4500000 | tf_op jit(solution)/shard_map/adam_attention/pallas_call | solution.py:455
  48.1 0.8 %finish.1 = (f32[800,128]{1,0:T(8,128)}, bf16[4,2,640]{2,1,0:T(2,128)(2,1)}) custom-call(f32[800,128]{1,0:T(8,128)S(1)} %get-tuple-element.6.master_in, bf16[8,640]{1,0:T(8,128)(2,1)S(1)} %get-tuple-element.7.mixed_in), custom_call_target="tpu_custom_call" | custom-call | tf_op jit(solution)/shard_map/finish/pallas_call | solution.py:506

commit v8 on v7

--- a/solution.py
+++ b/solution.py
@@ -78,8 +78,11 @@
     above = dev(lax.rem(z + 1, 8), y, 1 - r, t)
     below = dev(lax.rem(z + 7, 8), y, 1 - r, t)
 
+    def paired(d):
+        return lax.rem(yp + lax.div(d, 2), 2) * 2 + lax.rem(yy + lax.rem(d, 2), 2)
+
     def y_peer(d):
-        return dev(z, lax.rem(y + d, 4), r, t)
+        return dev(z, paired(jnp.int32(d)), r, t)
 
     def x_peer(e):
         return dev(z, y, r, lax.rem(xx + e, 4) * 2 + yh)
@@ -114,7 +117,7 @@
     lax.fori_loop(0, QPEERS, greet_q, 0)
     for e in (4, 3, 5, 2, 6, 1, 7, 0):
         there = lax.rem(t + e, 8)
-        device = dev(z, lax.rem(y + lax.div(there, 2), 4), r, there)
+        device = dev(z, paired(lax.div(there, 2)), r, there)
         if e == 0:
             pl.when(xx != 0)(functools.partial(greet, device))
         else:
@@ -252,14 +255,14 @@
     places = []
     for j in stored:
         k = lax.rem(z + 8 - lax.div(j, 8), 8)
-        source = lax.rem(lax.rem(lax.div(j, 2), 4) + 4 - y, 4)
+        source = paired(lax.rem(lax.div(j, 2), 4))
         rr = lax.rem(lax.rem(j, 2) + r, 2)
         slot = jnp.int32(0)
         for i in range(1, 8):
             slot = jnp.where(k == RING[i], i, slot)
         places.append(source * 16 + slot * 2 + rr)
     for xs_ in range(4):
-        source_y = lax.rem(y + xs_, 4)
+        source_y = paired(jnp.int32(xs_))
         for k in range(8):
             for rr in range(2):
                 j = (lax.rem(z + 8 - k, 8) * 4 + source_y) * 2 + lax.rem(r + rr, 2)
@@ -383,7 +386,7 @@
         pltpu.make_async_copy(s4.at[0], s4.at[0], r4_recv.at[e]).wait()
         summed = summed + r4[e].astype(F32)
     s5[...] = summed.astype(BF16)
-    target_y = lax.rem(y + 4 - xx, 4)
+    target_y = paired(xx)
 
     def to_owner(dx, flip):
         return pltpu.make_async_remote_copy(

time: 49.8 us -> 49.1 us (0.986); the launches traced: 48.8 us -> 48.9 us
  no operation moved by 1% of the time
where the time goes in v8:
time: 49.1 us; the launch traced here: 48.9 us
  Pallas kernels  48.3 us (98%)
  between operations  0.64 us (1%)
    pallas_call x1, Pallas kernels, body(): pl.pallas_call(kernel, out_shape=(pltpu.VMEM(flat, F32), pltpu.VMEM((TOKE...  47.5 us

profile of v8, /device:TPU:6, one launch (start us, length us, event | category | flops | bytes accessed | tf_op | source)
XLA Modules:
  0.0 48.9 jit_solution(962586820968231781)
XLA Ops:
  0.6 47.5 %adam_attention.1 = (f32[800,128]{1,0:T(8,128)S(1)}, bf16[8,640]{1,0:T(8,128)(2,1)S(1)}) custom-call(s32[64]{0:T(128)} %order_in.1, s32[2]{0:T(128)} %lengths_in.1, bf16[4,2,5120]{2,1,0:T(2,128)(2,1)} %x_in.1, f32[1,5120]{1,0:T(1,128)} %bitcast.14, f32[640]{0:T(1024)} %post_in.1, f32[1,128]{1,0:T(1,128)} %constant.2.clone.freq_in, f32[800,128]{1,0:T(8,128)} %bitcast.10, ...), custom_call_target="tpu_custom_call" | custom-call | flops 400000000 | bytes 4500000 | tf_op jit(solution)/shard_map/adam_attention/pallas_call | solution.py:458
  48.1 0.8 %finish.1 = (f32[800,128]{1,0:T(8,128)}, bf16[4,2,640]{2,1,0:T(2,128)(2,1)}) custom-call(f32[800,128]{1,0:T(8,128)S(1)} %get-tuple-element.6.master_in, bf16[8,640]{1,0:T(8,128)(2,1)S(1)} %get-tuple-element.7.mixed_in), custom_call_target="tpu_custom_call" | custom-call | tf_op jit(solution)/shard_map/finish/pallas_call | solution.py:509

commit v9 on v8

--- a/solution.py
+++ b/solution.py
@@ -107,14 +107,10 @@
     def greet(device):
         pl.semaphore_signal(barrier, inc=1, device_id=device, device_id_type=MESH)
 
-    def far_first(i):
-        return lax.rem(QPEERS // 2 + jnp.where(lax.rem(i, 2) == 1, lax.div(i + 1, 2), -lax.div(i, 2)), QPEERS)
-
-    def greet_q(i, carry):
-        greet(q_peer(far_first(i)))
-        return carry
-
-    lax.fori_loop(0, QPEERS, greet_q, 0)
+    far_first = [(QPEERS // 2 + ((i + 1) // 2 if i % 2 else -(i // 2))) % QPEERS for i in range(QPEERS)]
+
+    for d in far_first:
+        greet(q_peer(d))
     for e in (4, 3, 5, 2, 6, 1, 7, 0):
         there = lax.rem(t + e, 8)
         device = dev(z, paired(lax.div(there, 2)), r, there)
@@ -165,14 +161,10 @@
 
     pl.semaphore_wait(barrier, QPEERS + 7 + 6 + 3 + jnp.where(xx != 0, 1, 0))
 
-    def send_h(i, carry):
-        d = far_first(i)
+    for d in far_first:
         pltpu.make_async_remote_copy(
             src_ref=hs.at[d], dst_ref=hr.at[d], send_sem=h_send, recv_sem=h_recv, device_id=q_peer(d), device_id_type=MESH
         ).start()
-        return carry
-
-    lax.fori_loop(0, QPEERS, send_h, 0)
     pending.append(pltpu.make_async_copy(hs, hs, h_send).wait)
 
     def share(src, dst, device):
@@ -282,9 +274,7 @@
     ps2[...] = jnp.concatenate([partial[:, :, 512:640], partial[:, :, 640:]], axis=1).astype(BF16)
 
     for source, target, left_sem, got_sem in ((ps, pr, p_send, p_recv), (ps2, pr2, p2_send, p2_recv)):
-
-        def send_p(i, carry):
-            d = far_first(i)
+        for d in far_first:
             pltpu.make_async_remote_copy(
                 src_ref=source.at[d],
                 dst_ref=target.at[d],
@@ -293,9 +283,6 @@
                 device_id=q_peer(QPEERS - d),
                 device_id_type=MESH,
             ).start()
-            return carry
-
-        lax.fori_loop(0, QPEERS, send_p, 0)
         pending.append(pltpu.make_async_copy(source, source, left_sem).wait)
     ring_advance()
     ring_advance()

time: 49.1 us -> 48.6 us (0.990)
  no operation moved by 1% of the time
where the time goes in v9:
time: 48.6 us; the launch traced here: 48.5 us
  Pallas kernels  47.9 us (99%)
  between operations  0.64 us (1%)
    pallas_call x1, Pallas kernels, body(): pl.pallas_call(kernel, out_shape=(pltpu.VMEM(flat, F32), pltpu.VMEM((TOKE...  47.1 us

profile of v9, /device:TPU:6, one launch (start us, length us, event | category | flops | bytes accessed | tf_op | source)
XLA Modules:
  0.0 48.5 jit_solution(3602965801408023319)
XLA Ops:
  0.6 47.1 %adam_attention.1 = (f32[800,128]{1,0:T(8,128)S(1)}, bf16[8,640]{1,0:T(8,128)(2,1)S(1)}) custom-call(s32[64]{0:T(128)} %order_in.1, s32[2]{0:T(128)} %lengths_in.1, bf16[4,2,5120]{2,1,0:T(2,128)(2,1)} %x_in.1, f32[1,5120]{1,0:T(1,128)} %bitcast.14, f32[640]{0:T(1024)} %post_in.1, f32[1,128]{1,0:T(1,128)} %constant.2.clone.freq_in, f32[800,128]{1,0:T(8,128)} %bitcast.10, ...), custom_call_target="tpu_custom_call" | custom-call | flops 400000000 | bytes 4500000 | tf_op jit(solution)/shard_map/adam_attention/pallas_call | solution.py:445
  47.7 0.8 %finish.1 = (f32[800,128]{1,0:T(8,128)}, bf16[4,2,640]{2,1,0:T(2,128)(2,1)}) custom-call(f32[800,128]{1,0:T(8,128)S(1)} %get-tuple-element.6.master_in, bf16[8,640]{1,0:T(8,128)(2,1)S(1)} %get-tuple-element.7.mixed_in), custom_call_target="tpu_custom_call" | custom-call | tf_op jit(solution)/shard_map/finish/pallas_call | solution.py:496

commit v10 on v9

--- a/solution.py
+++ b/solution.py
@@ -161,10 +161,13 @@
 
     pl.semaphore_wait(barrier, QPEERS + 7 + 6 + 3 + jnp.where(xx != 0, 1, 0))
 
-    for d in far_first:
-        pltpu.make_async_remote_copy(
-            src_ref=hs.at[d], dst_ref=hr.at[d], send_sem=h_send, recv_sem=h_recv, device_id=q_peer(d), device_id_type=MESH
-        ).start()
+    def send_h(ds):
+        for d in ds:
+            pltpu.make_async_remote_copy(
+                src_ref=hs.at[d], dst_ref=hr.at[d], send_sem=h_send, recv_sem=h_recv, device_id=q_peer(d), device_id_type=MESH
+            ).start()
+
+    send_h(far_first[:9])
     pending.append(pltpu.make_async_copy(hs, hs, h_send).wait)
 
     def share(src, dst, device):
@@ -226,6 +229,7 @@
     for part in range(2):
         up[0, part].start()
         down[0, part].start()
+    send_h(far_first[9:])
     to_twin[0].start()
 
     loads[9].wait()

time: 48.6 us -> 49.4 us (1.016)
  Pallas kernels: 47.9 us -> 48.6 us
    pallas_call x1, Pallas kernels: 47.1 us -> 47.9 us  [body(): pl.pallas_call(kernel, out_shape=(pltpu.VMEM(flat, F32), pltpu.VMEM((TOKE...]
where the time goes in v10:
time: 49.4 us; the launch traced here: 49.3 us
  Pallas kernels  48.6 us (98%)
  between operations  0.64 us (1%)
    pallas_call x1, Pallas kernels, body(): pl.pallas_call(kernel, out_shape=(pltpu.VMEM(flat, F32), pltpu.VMEM((TOKE...  47.9 us

profile of v10, /device:TPU:6, one launch (start us, length us, event | category | flops | bytes accessed | tf_op | source)
XLA Modules:
  0.0 49.3 jit_solution(8233779679446384011)
XLA Ops:
  0.6 47.9 %adam_attention.1 = (f32[800,128]{1,0:T(8,128)S(1)}, bf16[8,640]{1,0:T(8,128)(2,1)S(1)}) custom-call(s32[64]{0:T(128)} %order_in.1, s32[2]{0:T(128)} %lengths_in.1, bf16[4,2,5120]{2,1,0:T(2,128)(2,1)} %x_in.1, f32[1,5120]{1,0:T(1,128)} %bitcast.14, f32[640]{0:T(1024)} %post_in.1, f32[1,128]{1,0:T(1,128)} %constant.2.clone.freq_in, f32[800,128]{1,0:T(8,128)} %bitcast.10, ...), custom_call_target="tpu_custom_call" | custom-call | flops 400000000 | bytes 4500000 | tf_op jit(solution)/shard_map/adam_attention/pallas_call | solution.py:449
  48.5 0.8 %finish.1 = (f32[800,128]{1,0:T(8,128)}, bf16[4,2,640]{2,1,0:T(2,128)(2,1)}) custom-call(f32[800,128]{1,0:T(8,128)S(1)} %get-tuple-element.6.master_in, bf16[8,640]{1,0:T(8,128)(2,1)S(1)} %get-tuple-element.7.mixed_in), custom_call_target="tpu_custom_call" | custom-call | tf_op jit(solution)/shard_map/finish/pallas_call | solution.py:500
